TPU v7x, 512 devices: a whole 4x8x8 slice. The times are simulated.
512 devices in a mesh: slab: 32 (over x_hi, z, core), grp: 16 (over y, x_lo).
Axes of the slice: x: 4 (x_hi: 2, x_lo: 2; x = x_hi * 2 + x_lo), y: 8, z: 8, core: 2. Of those that a mesh axis runs over, the one named last changes fastest.
Arguments:
- comp: float32 [4096, 128, 128], P(('slab', 'grp')), may hold values from -1 to 1
- guess: float32 [1024, 32, 32], P('slab', 'grp'), may hold values from -3 to 3
Outputs:
- comp_next: float32 [4096, 128, 128], P(('slab', 'grp'))
- potential: float32 [1024, 32, 32], P('slab', 'grp')
All inputs are finite; a program needn't handle non-finite values.
Results may differ from a plain program's by a relative error of at most 0.00002.
Values sent between devices are 32-bit elements; how exact they have to be, the bound alone decides.
A program may use at most 64 MiB of HBM per device.

v0:
```python
import jax
import jax.numpy as jnp
from jax import lax
from jax.sharding import PartitionSpec as P

NPRE = 1
NCOARSE = 3
NPOST = 2


gradient_energy = 0.5
screening = 0.5
damping = 0.8
long_range = 4.0
time_step = 0.02


def laid_out(tiles, dim):
    tiles = jnp.moveaxis(tiles, 0, dim)
    dims = tiles.shape
    return tiles.reshape(*dims[:dim], dims[dim] * dims[dim + 1], *dims[dim + 2 :])


def gather_together(arrays, axis, dims):
    ravelled = jnp.concatenate([a.reshape(-1) for a in arrays])
    lines, at, done = (lax.all_gather(ravelled, axis), 0, [])
    for a, dim in zip(arrays, dims):
        tiles = lines[:, at : at + a.size].reshape(-1, *a.shape)
        done.append(laid_out(tiles, dim))
        at += a.size
    return tuple(done)


def extended_2(block, sides, width):
    for axis, dim in sides:
        count = lax.axis_size(axis)
        forward = [(i, i + 1) for i in range(count - 1)]
        backward = [(target, source) for source, target in forward]
        low = lax.ppermute(
            lax.slice_in_dim(block, block.shape[dim] - width, None, axis=dim), axis, forward
        )
        high = lax.ppermute(lax.slice_in_dim(block, 0, width, axis=dim), axis, backward)
        block = jnp.concatenate([low, block, high], axis=dim)
    return block


def padded_2(array, sides, width):
    edges = {}
    for axis, dim in sides:
        peers, length = (lax.axis_size(axis), array.shape[dim])
        up = [(i, (i + 1) % peers) for i in range(peers - 1)]
        last = lax.slice_in_dim(array, length - width, length, axis=dim)
        leading = lax.slice_in_dim(array, 0, width, axis=dim)
        edges[dim] = (
            lax.ppermute(last, axis, up),
            lax.ppermute(leading, axis, [(b, a) for a, b in up]),
        )
    done = []
    for _, dim in sides:
        low, high = edges[dim]
        around = [(width, width) if d in done else (0, 0) for d in range(array.ndim)]
        array = jnp.concatenate([jnp.pad(low, around), array, jnp.pad(high, around)], axis=dim)
        done.append(dim)
    return array


def laplace_padded(padded):
    inner = padded[1:-1, 1:-1, 1:-1]
    beside_all = padded[2:, 1:-1, 1:-1] + padded[:-2, 1:-1, 1:-1]
    beside_all = beside_all + padded[1:-1, 2:, 1:-1] + padded[1:-1, :-2, 1:-1]
    beside_all = beside_all + padded[1:-1, 1:-1, 2:] + padded[1:-1, 1:-1, :-2]
    return beside_all - 6.0 * inner


def pad_across(field):
    return jnp.pad(field, ((0, 0), (1, 1), (1, 1)))


def block_mean(field, factor):
    first, second, third = field.shape
    return field.reshape(
        first // factor, factor, second // factor, factor, third // factor, factor
    ).mean(axis=(1, 3, 5))


def expand(field, factor):
    first, second, third = field.shape
    wide = jnp.broadcast_to(
        field[:, None, :, None, :, None], (first, factor, second, factor, third, factor)
    )
    return wide.reshape(first * factor, second * factor, third * factor)


def keep_inside(field, first_plane, total_planes):
    plane_ids = first_plane + jnp.arange(field.shape[0], dtype=jnp.int32)
    inside = (plane_ids >= 0) & (plane_ids < total_planes)
    return jnp.where(inside[:, None, None], field, jnp.float32(0.0))


def shrink_sweep(potential, source, first_plane, total_planes):
    operated = screening * potential[1:-1] - laplace_padded(pad_across(potential))
    updated = potential[1:-1] + damping * (source[1:-1] - operated) / (screening + 6.0)
    return (keep_inside(updated, first_plane + 1, total_planes), source[1:-1], first_plane + 1)


def deep_cycle(source, guess):
    local_planes = source.shape[0]
    local_rows = guess.shape[1]
    block, start = gather_together((source, guess), "grp", (0, 1))
    group_planes = block.shape[0]
    depth = NPRE + NPOST + 2 * NCOARSE - 1
    total_planes = lax.axis_size("slab") * group_planes
    wide_source, wide_pot = (
        extended_2(block, (("slab", 0),), depth),
        extended_2(start, (("slab", 0),), depth),
    )
    first_plane = lax.axis_index("slab") * group_planes - depth
    wide_pot, wide_source, first_plane = shrink_sweep(
        wide_pot, wide_source, first_plane, total_planes
    )
    operated = screening * wide_pot[1:-1] - laplace_padded(pad_across(wide_pot))
    residual = keep_inside(wide_source[1:-1] - operated, first_plane + 1, total_planes)
    wide_pot = wide_pot[1:-1]
    wide_source = wide_source[1:-1]
    first_plane = first_plane + 1
    coarsest = block_mean(residual, 2)
    coarse_first = first_plane // 2
    coarse_total = total_planes // 2
    correction = damping * coarsest / (screening + 1.5)
    for sweep in range(NCOARSE - 1):
        operated = screening * correction[1:-1] - 0.25 * laplace_padded(pad_across(correction))
        correction = correction[1:-1] + damping * (coarsest[1:-1] - operated) / (screening + 1.5)
        coarse_first = coarse_first + 1
        correction = keep_inside(correction, coarse_first, coarse_total)
        coarsest = coarsest[1:-1]
    cut = 2 * (NCOARSE - 1)
    wide_pot = wide_pot[cut:-cut] + expand(correction, 2)
    wide_source = wide_source[cut:-cut]
    first_plane = first_plane + cut
    for sweep in range(NPOST):
        wide_pot, wide_source, first_plane = shrink_sweep(
            wide_pot, wide_source, first_plane, total_planes
        )
    potential = lax.dynamic_slice_in_dim(
        wide_pot, lax.axis_index("grp") * local_rows, local_rows, 1
    )
    slab_planes = lax.dynamic_slice_in_dim(
        wide_pot, lax.axis_index("grp") * local_planes, local_planes, 0
    )
    return (potential, slab_planes)


def per_device(comp, guess):
    extended = padded_2(comp, ((("slab", "grp"), 0),), 1)
    chem = comp * comp * comp - comp - gradient_energy * laplace_padded(pad_across(extended))
    source = block_mean(comp, 4)
    potential, slab_planes = deep_cycle(source, guess)
    field = chem + long_range * expand(slab_planes, 4)
    extended = padded_2(field, ((("slab", "grp"), 0),), 1)
    comp_next = comp + time_step * laplace_padded(pad_across(extended))
    return (comp_next, potential)


def solution(mesh):
    placed = (P(("slab", "grp"), None, None), P("slab", "grp", None))
    return jax.shard_map(
        per_device,
        mesh=mesh,
        in_specs=placed,
        out_specs=(P(("slab", "grp"), None, None), P("slab", "grp", None)),
        check_vma=False,
    )
```

profile of v0, /device:TPU:4, one launch (start us, length us, event | category | flops | bytes accessed | tf_op | source)
XLA Modules:
  0.0 158.8 jit_solution(3005524916497095743)
XLA Ops:
  0.6 19.5 %reshape.77 = f32[2,4,32,4,32,4]{5,4,3,2,1,0:T(8,128)} reshape(f32[8,128,128]{2,1,0:T(8,128)} %param.2) | data formatting | bytes 1048576 | tf_op jit(solution)/shard_map/reshape | solution.py:81
  20.1 7.1 %reduce_sum.18 = f32[2,32,32]{2,1,0:T(8,128)S(1)} reduce(f32[2,4,32,4,32,4]{5,4,3,2,1,0:T(8,128)} %reshape.77, f32[]{:T(128)} %constant.36.clone.1), dimensions={1,3,5}, to_apply=%region_0.1 | reduce | flops 129024 | bytes 532484 | tf_op jit(solution)/shard_map/reduce_sum | solution.py:83
  27.2 0.1 div.60
  27.3 0.1 reshape.78
  27.3 35.0 %all-gather = f32[65536]{0:T(1024)S(1)} all-gather(f32[4096]{0:T(1024)S(1)} %pad_maximum_fusion.4), channel_id=2, replica_groups=mesh['slab'=32,'grp'=16] {'grp'}, dimensions={0}, use_global_device_ids=true | all-gather | bytes 278528 | tf_op jit(solution)/shard_map/all_gather | solution.py:26
  62.3 0.1 reshape.83
  62.4 0.0 copy-start
  62.4 0.4 reshape.79
  63.0 1.9 %collective-permute-start.2 = (f32[8,32,32]{2,1,0:T(8,128)S(1)}, f32[8,32,32]{2,1,0:T(8,128)S(1)}, u32[]{:S(2)}, u32[]{:S(2)}) collective-permute-start(f32[8,32,32]{2,1,0:T(8,128)S(1)} %copy.34), channel_id=1, source_target_pairs={{0,16},{16,32},{32,48},{48,64},{64,80},{80,96},{96,112},{112,128},... | collective-permute-start | bytes 98312 | tf_op jit(solution)/shard_map/ppermute | solution.py:39
  65.0 7.3 %collective-permute-start.3 = (f32[8,32,32]{2,1,0:T(8,128)S(1)}, f32[8,32,32]{2,1,0:T(8,128)S(1)}, u32[]{:S(2)}, u32[]{:S(2)}) collective-permute-start(f32[8,32,32]{2,1,0:T(8,128)S(1)} %copy.37), channel_id=1, source_target_pairs={{16,0},{32,16},{48,32},{64,48},{80,64},{96,80},{112,96},{128,112},... | collective-permute-start | bytes 98312 | tf_op jit(solution)/shard_map/ppermute | solution.py:42
  72.2 0.1 slice.293
  72.3 1.9 %collective-permute-start.4 = (f32[8,32,32]{2,1,0:T(8,128)S(1)}, f32[8,32,32]{2,1,0:T(8,128)}, u32[]{:S(2)}, u32[]{:S(2)}) collective-permute-start(f32[8,32,32]{2,1,0:T(8,128)S(1)} %slice.293), channel_id=1, source_target_pairs={{0,16},{16,32},{32,48},{48,64},{64,80},{80,96},{96,112},{112,128},... | collective-permute-start | bytes 98312 | tf_op jit(solution)/shard_map/ppermute | solution.py:39
  74.3 0.1 slice.296
  74.4 7.3 %collective-permute-start.5 = (f32[8,32,32]{2,1,0:T(8,128)S(1)}, f32[8,32,32]{2,1,0:T(8,128)S(1)}, u32[]{:S(2)}, u32[]{:S(2)}) collective-permute-start(f32[8,32,32]{2,1,0:T(8,128)S(1)} %slice.296), channel_id=1, source_target_pairs={{16,0},{32,16},{48,32},{64,48},{80,64},{96,80},{112,96},{128,112},... | collective-permute-start | bytes 98312 | tf_op jit(solution)/shard_map/ppermute | solution.py:42
  81.6 0.6 fusion.73
  82.3 1.9 %collective-permute-start = (f32[1,128,128]{2,1,0:T(8,128)}, f32[1,128,128]{2,1,0:T(8,128)S(1)}, u32[]{:S(2)}, u32[]{:S(2)}) collective-permute-start(f32[1,128,128]{2,1,0:T(8,128)} %get-tuple-element.11), channel_id=1, source_target_pairs={{1,0},{2,1},{3,2},{4,3},{5,4},{6,5},{7,6},{8,7},{9,8},{10,9},{11,1... | collective-permute-start | bytes 196616 | tf_op jit(solution)/shard_map/ppermute | solution.py:56
  84.3 0.1 copy.35
  84.4 0.2 reshape_reshape.3
  84.6 4.1 %collective-permute-start.1 = (f32[1,128,128]{2,1,0:T(8,128)S(1)}, f32[1,128,128]{2,1,0:T(8,128)S(1)}, u32[]{:S(2)}, u32[]{:S(2)}) collective-permute-start(f32[1,128,128]{2,1,0:T(8,128)S(1)} %get-tuple-element.10), channel_id=1, source_target_pairs={{0,1},{1,2},{2,3},{3,4},{4,5},{5,6},{6,7},{7,8},{8,9},{9,10},{10,1... | collective-permute-start | bytes 196616 | tf_op jit(solution)/shard_map/ppermute | solution.py:55
  88.7 0.3 copy_dynamic-update-slice_fusion
  89.0 0.0 collective-permute-done.4
  89.0 0.9 constant_dynamic-update-slice_fusion.4
  90.0 0.0 collective-permute-done.3
  90.0 0.0 collective-permute-done.5
  90.0 0.7 fusion.12
  90.8 0.6 fusion.20
  91.4 8.0 %reshape.81 = f32[22,2,16,2,16,2]{5,4,3,2,1,0:T(8,128)} reshape(f32[44,32,32]{2,1,0:T(8,128)S(1)} %fusion.20) | data formatting | bytes 360448 | tf_op jit(solution)/shard_map/reshape | solution.py:81
  99.4 5.2 %reduce_sum.19 = f32[22,16,16]{2,1,0:T(8,128)S(1)} reduce(f32[22,2,16,2,16,2]{5,4,3,2,1,0:T(8,128)} %reshape.81, f32[]{:T(128)} %constant.36.clone.1), dimensions={1,3,5}, to_apply=%region_1.2 | reduce | flops 39424 | bytes 202756 | tf_op jit(solution)/shard_map/reduce_sum | solution.py:83
  104.6 0.2 fusion.60
  104.8 0.2 fusion.71
  104.9 4.3 %broadcast_in_dim.100 = f32[18,2,16,2,16,2]{5,4,3,2,1,0:T(8,128)} broadcast(f32[18,16,16]{2,1,0:T(8,128)S(1)} %fusion.71), dimensions={0,2,4} | broadcast | bytes 165888 | tf_op jit(solution)/shard_map/broadcast_in_dim | solution.py:88
  109.3 7.0 %reshape.82 = f32[36,32,32]{2,1,0:T(8,128)S(1)} reshape(f32[18,2,16,2,16,2]{5,4,3,2,1,0:T(8,128)} %broadcast_in_dim.100) | data formatting | bytes 294912 | tf_op jit(solution)/shard_map/reshape | solution.py:91
  116.3 0.1 slice_add_fusion.2
  116.4 0.5 fusion.30
  117.0 0.5 fusion.40
  117.5 8.0 %broadcast_in_dim.103 = f32[2,4,32,4,32,4]{5,4,3,2,1,0:T(8,128)} broadcast(f32[2,32,32]{2,1,0:T(8,128)S(1)} %dynamic-slice_multiply_fusion), dimensions={0,2,4} | broadcast | bytes 532480 | tf_op jit(solution)/shard_map/broadcast_in_dim | solution.py:88
  125.5 14.8 %mul.174 = f32[8,128,128]{2,1,0:T(8,128)S(1)} reshape(f32[2,4,32,4,32,4]{5,4,3,2,1,0:T(8,128)} %broadcast_in_dim.103) | data formatting | bytes 1048576 | tf_op jit(solution)/shard_map/mul | solution.py:158
  140.2 0.0 collective-permute-done
  140.3 0.0 collective-permute-done.1
  140.3 0.4 select_maximum_fusion.2
  140.7 0.6 fusion.42
  141.4 5.9 %collective-permute-start.6 = (f32[1,128,128]{2,1,0:T(8,128)S(1)}, f32[1,128,128]{2,1,0:T(8,128)S(1)}, u32[]{:S(2)}, u32[]{:S(2)}) collective-permute-start(f32[1,128,128]{2,1,0:T(8,128)S(1)} %get-tuple-element.9), channel_id=1, source_target_pairs={{1,0},{2,1},{3,2},{4,3},{5,4},{6,5},{7,6},{8,7},{9,8},{10,9},{11,1... | collective-permute-start | bytes 196616 | tf_op jit(solution)/shard_map/ppermute | solution.py:56
  147.2 1.9 %collective-permute-start.7 = (f32[1,128,128]{2,1,0:T(8,128)S(1)}, f32[1,128,128]{2,1,0:T(8,128)S(1)}, u32[]{:S(2)}, u32[]{:S(2)}) collective-permute-start(f32[1,128,128]{2,1,0:T(8,128)S(1)} %get-tuple-element.8), channel_id=1, source_target_pairs={{0,1},{1,2},{2,3},{3,4},{4,5},{5,6},{6,7},{7,8},{8,9},{9,10},{10,1... | collective-permute-start | bytes 196616 | tf_op jit(solution)/shard_map/ppermute | solution.py:55
  149.2 0.6 constant_dynamic-slice_fusion
  149.8 0.0 collective-permute-done.6
  149.8 7.2 %collective-permute-done.7 = f32[1,128,128]{2,1,0:T(8,128)S(1)} collective-permute-done((f32[1,128,128]{2,1,0:T(8,128)S(1)}, f32[1,128,128]{2,1,0:T(8,128)S(1)}, u32[]{:S(2)}, u32[]{:S(2)}) %collective-permute-start.7) | collective-permute-done | bytes 65568 | tf_op jit(solution)/shard_map/ppermute | solution.py:55
  157.0 0.4 select_maximum_fusion
  157.5 1.3 fusion.45
  (26 shorter events, 0.3 us)
Async XLA Ops:
  20.1 7.2 %copy-start.1 = (f32[32,2,32]{2,1,0:T(2,128)S(1)}, f32[32,2,32]{2,1,0:T(2,128)}, u32[]{:S(2)}) copy-start(f32[32,2,32]{2,1,0:T(2,128)} %param.3) | copy-start | bytes 24580
  62.4 19.2 %copy-start = (f32[8,128,128]{2,1,0:T(8,128)S(1)}, f32[8,128,128]{2,1,0:T(8,128)}, u32[]{:S(2)}) copy-start(f32[8,128,128]{2,1,0:T(8,128)} %param.2) | copy-start | bytes 1572868
  63.0 21.6 %collective-permute-start.2 = (f32[8,32,32]{2,1,0:T(8,128)S(1)}, f32[8,32,32]{2,1,0:T(8,128)S(1)}, u32[]{:S(2)}, u32[]{:S(2)}) collective-permute-start(f32[8,32,32]{2,1,0:T(8,128)S(1)} %copy.34), channel_id=1, source_target_pairs={{0,16},{16,32},{32,48},{48,64},{64,80},{80,96},{96,112},{112,128},... | collective-permute-start | bytes 98312 | tf_op jit(solution)/shard_map/ppermute | solution.py:39
  65.0 25.0 %collective-permute-start.3 = (f32[8,32,32]{2,1,0:T(8,128)S(1)}, f32[8,32,32]{2,1,0:T(8,128)S(1)}, u32[]{:S(2)}, u32[]{:S(2)}) collective-permute-start(f32[8,32,32]{2,1,0:T(8,128)S(1)} %copy.37), channel_id=1, source_target_pairs={{16,0},{32,16},{48,32},{64,48},{80,64},{96,80},{112,96},{128,112},... | collective-permute-start | bytes 98312 | tf_op jit(solution)/shard_map/ppermute | solution.py:42
  72.3 16.7 %collective-permute-start.4 = (f32[8,32,32]{2,1,0:T(8,128)S(1)}, f32[8,32,32]{2,1,0:T(8,128)}, u32[]{:S(2)}, u32[]{:S(2)}) collective-permute-start(f32[8,32,32]{2,1,0:T(8,128)S(1)} %slice.293), channel_id=1, source_target_pairs={{0,16},{16,32},{32,48},{48,64},{64,80},{80,96},{96,112},{112,128},... | collective-permute-start | bytes 98312 | tf_op jit(solution)/shard_map/ppermute | solution.py:39
  74.4 15.7 %collective-permute-start.5 = (f32[8,32,32]{2,1,0:T(8,128)S(1)}, f32[8,32,32]{2,1,0:T(8,128)S(1)}, u32[]{:S(2)}, u32[]{:S(2)}) collective-permute-start(f32[8,32,32]{2,1,0:T(8,128)S(1)} %slice.296), channel_id=1, source_target_pairs={{16,0},{32,16},{48,32},{64,48},{80,64},{96,80},{112,96},{128,112},... | collective-permute-start | bytes 98312 | tf_op jit(solution)/shard_map/ppermute | solution.py:42
  82.3 58.0 %collective-permute-start = (f32[1,128,128]{2,1,0:T(8,128)}, f32[1,128,128]{2,1,0:T(8,128)S(1)}, u32[]{:S(2)}, u32[]{:S(2)}) collective-permute-start(f32[1,128,128]{2,1,0:T(8,128)} %get-tuple-element.11), channel_id=1, source_target_pairs={{1,0},{2,1},{3,2},{4,3},{5,4},{6,5},{7,6},{8,7},{9,8},{10,9},{11,1... | collective-permute-start | bytes 196616 | tf_op jit(solution)/shard_map/ppermute | solution.py:56
  84.6 55.7 %collective-permute-start.1 = (f32[1,128,128]{2,1,0:T(8,128)S(1)}, f32[1,128,128]{2,1,0:T(8,128)S(1)}, u32[]{:S(2)}, u32[]{:S(2)}) collective-permute-start(f32[1,128,128]{2,1,0:T(8,128)S(1)} %get-tuple-element.10), channel_id=1, source_target_pairs={{0,1},{1,2},{2,3},{3,4},{4,5},{5,6},{6,7},{7,8},{8,9},{9,10},{10,1... | collective-permute-start | bytes 196616 | tf_op jit(solution)/shard_map/ppermute | solution.py:55
  141.4 8.4 %collective-permute-start.6 = (f32[1,128,128]{2,1,0:T(8,128)S(1)}, f32[1,128,128]{2,1,0:T(8,128)S(1)}, u32[]{:S(2)}, u32[]{:S(2)}) collective-permute-start(f32[1,128,128]{2,1,0:T(8,128)S(1)} %get-tuple-element.9), channel_id=1, source_target_pairs={{1,0},{2,1},{3,2},{4,3},{5,4},{6,5},{7,6},{8,7},{9,8},{10,9},{11,1... | collective-permute-start | bytes 196616 | tf_op jit(solution)/shard_map/ppermute | solution.py:56
  147.2 9.8 %collective-permute-start.7 = (f32[1,128,128]{2,1,0:T(8,128)S(1)}, f32[1,128,128]{2,1,0:T(8,128)S(1)}, u32[]{:S(2)}, u32[]{:S(2)}) collective-permute-start(f32[1,128,128]{2,1,0:T(8,128)S(1)} %get-tuple-element.8), channel_id=1, source_target_pairs={{0,1},{1,2},{2,3},{3,4},{4,5},{5,6},{6,7},{7,8},{8,9},{9,10},{10,1... | collective-permute-start | bytes 196616 | tf_op jit(solution)/shard_map/ppermute | solution.py:55
where the time goes:
time: 159 us
  local copies, waits for them, and re-layouts  65.3 us (41%)
  blocking collectives  35 us (22%)
  starting transfers between devices  32.1 us (20%)
  other arithmetic  17.9 us (11%)
  waiting for transfers between devices  7.25 us (5%)
    all_gather x1, blocking collectives, gather_together(): lines, at, done = (lax.all_gather(ravelled, axis), 0, [])  35 us
    reshape x2, local copies, waits for them, and re-layouts, block_mean(): field.reshape(first // factor, factor, second // factor, factor, third //...  27.5 us
    mul x1, local copies, waits for them, and re-layouts, per_device(): field = chem + long_range * expand(slab_planes, 4)  14.8 us
    ppermute x2, starting transfers between devices, extended_2(): lax.ppermute(lax.slice_in_dim(block, 0, width, axis=dim), axis, backward)  14.5 us
    broadcast_in_dim x2, local copies, waits for them, and re-layouts, expand(): jnp.broadcast_to(field[:, None, :, None, :, None], (first, factor, second...  12.3 us
    reduce_sum x2, other arithmetic, block_mean(): return field.reshape(first // factor, factor, second // factor, factor, t...  12.2 us
    ppermute x2, starting transfers between devices, padded_2(): lax.ppermute(leading, axis, [(b, a) for a, b in up])  7.77 us
    ppermute x2, waiting for transfers between devices, padded_2(): lax.ppermute(last, axis, up)  7.23 us
  transfers between devices with their start and end apart: 8, of which 1 were waited for; matrix products, arithmetic and copies ran while one was open for 34% of the time, Pallas kernels for 0%

commit v1 on v0

v1 whole, which is shorter than its diff:
```python
import jax
import jax.numpy as jnp
from jax import lax
from jax.experimental import pallas as pl
from jax.experimental.pallas import tpu as pltpu
from jax.sharding import PartitionSpec as P

MESH = pl.DeviceIdType.MESH
REACH = 5
WINDOW = 2 * REACH + 1
F32 = jnp.float32
BF16 = jnp.bfloat16


def iota(shape, dim):
    return lax.broadcasted_iota(jnp.int32, shape, dim)


def lanes(x, shift):
    return pltpu.roll(x, (-shift) % 128, 1)


def rows(x, shift):
    return pltpu.roll(x, (-shift) % x.shape[0], 0)


def split3(x):
    high = x.astype(BF16)
    rest = x - high.astype(F32)
    mid = rest.astype(BF16)
    low = (rest - mid.astype(F32)).astype(BF16)
    return high, mid, low


def neighbours(v, first, last):
    own = v[16:-16]
    lane, row = iota(own.shape, 1), iota(own.shape, 0) % 16
    a, b = lanes(own, 32), lanes(own, -32)
    up = jnp.where(row < 15, rows(b, 1), 0.0)
    down = jnp.where(row > 0, rows(a, -1), 0.0)
    total = jnp.where(lane % 64 < 32, a + down, b + up)
    total += jnp.where(lane % 32 < 31, lanes(own, 1), 0.0)
    total += jnp.where(lane % 32 > 0, lanes(own, -1), 0.0)
    h = pltpu.roll(v, 64, 1)
    return total + h[16:-16] + jnp.where(lane < 64, h[:-32], h[32:])


def coarse_cycle(source, guess, first_pair, pairs):
    def inside(v, first):
        pair = first_pair + first + iota(v.shape, 0) // 16
        return jnp.where((pair >= 0) & (pair < pairs), v, 0.0)

    def sweep(v, s):
        return 0.2 * v[16:-16] + (0.8 / 6.5) * (s + neighbours(v, 0, 0))

    guess = inside(guess, 0)
    source = inside(source, 0)
    edge = jnp.zeros((16, 128), F32)
    pre = inside(sweep(jnp.concatenate([edge, guess, edge], 0), source), 0)
    resid = inside(source[16:-16] + neighbours(pre, 0, 0) - 6.5 * pre[16:-16], 1)
    lane = iota(resid.shape, 1)
    t = resid + pltpu.roll(resid, 64, 1)
    t = t + jnp.where(lane % 64 < 32, lanes(t, 32), lanes(t, -32))
    t = t + jnp.where(lane % 2 < 1, lanes(t, 1), lanes(t, -1))
    start = t * 0.05
    c, first = start, 1
    for _ in range(2):
        own = c[16:-16]
        lane, row = iota(own.shape, 1) % 32, iota(own.shape, 0) % 16
        total = c[:-32] + c[32:]
        total += jnp.where(row < 15, rows(own, 1), 0.0) + jnp.where(row > 0, rows(own, -1), 0.0)
        total += jnp.where(lane < 30, lanes(own, 2), 0.0) + jnp.where(lane > 1, lanes(own, -2), 0.0)
        first = first + 1
        c = inside(0.2 * own + start[16 * (first - 1) : -16 * (first - 1)] + 0.1 * total, first)
    mid = inside(pre[16 * first : -16 * first] + c, first)
    mid = inside(sweep(mid, source[16 * (first + 1) : -16 * (first + 1)]), first + 1)
    edge = jnp.zeros((16, 128), F32)
    mid = jnp.concatenate([edge, mid, edge], 0)
    return inside(sweep(mid, source[16 * (first + 1) : -16 * (first + 1)]), first + 1)


def plane_neighbours(v):
    row, lane = iota(v.shape, 0), iota(v.shape, 1)
    total = jnp.where(row < 127, rows(v, 1), 0.0) + jnp.where(row > 0, rows(v, -1), 0.0)
    total += jnp.where(lane < 127, lanes(v, 1), 0.0) + jnp.where(lane > 0, lanes(v, -1), 0.0)
    return total


def spread(fine, coarse):
    block, place = fine // 4, fine % 4
    same = jnp.where(block == coarse, 1.0, 0.0)
    first, last = jnp.where(place == 0, 1.0, 0.0), jnp.where(place == 3, 1.0, 0.0)
    second = -same * (first + last)
    second += first * jnp.where(block - 1 == coarse, 1.0, 0.0)
    second += last * jnp.where(block + 1 == coarse, 1.0, 0.0)
    return same, second


def step(
    slabs, comp, guess, out, pot, cells, given, lines, window, chem, sums, gather, z_mat, y_mat,
    potline, cell_sem, given_sem, line_send, line_recv, near_send, near_recv, halo_send,
    halo_recv, pot_send, pot_recv,
):
    s, g = lax.axis_index("slab"), lax.axis_index("grp")
    me = s * 16 + g
    pairs = slabs * 16

    def device(d):
        return (d // 16, d % 16)

    halves = [
        pltpu.make_async_copy(comp.at[4 * h : 4 * h + 4], cells.at[2 + 4 * h : 6 + 4 * h], cell_sem.at[h])
        for h in range(2)
    ]
    load_guess = pltpu.make_async_copy(guess, given, given_sem)
    load_guess.start()
    for half in halves:
        half.start()

    barrier = pltpu.get_barrier_semaphore()
    crossing = jnp.int32(15)
    for k in range(1, REACH + 1):
        for d, across in ((me + k, g + k > 15), (me - k, g - k < 0)):
            other = across & (d >= 0) & (d < pairs)
            crossing += other.astype(jnp.int32)

            @pl.when(other)
            def _():
                pl.semaphore_signal(barrier, 1, device_id=device(d), device_id_type=MESH)

    for k in range(1, 16):
        pl.semaphore_signal(barrier, 1, device_id=(s, (g + k) % 16), device_id_type=MESH)

    load_guess.wait()
    packed = given.reshape(64, 32)
    lines[...] = jnp.concatenate([packed[pl.ds(k, 16, stride=4), :] for k in range(4)], axis=1)

    pl.semaphore_wait(barrier, crossing)
    for k in range(1, 16):
        to = (g + k) % 16
        pltpu.make_async_remote_copy(
            lines.at[pl.ds(to, 1)], window.at[REACH, 1, pl.ds(g, 1)], line_send, line_recv,
            device_id=(s, to), device_id_type=MESH,
        ).start()
    window[REACH, 1, pl.ds(g, 1), :] = lines[pl.ds(g, 1), :]

    at, lane = iota((512, 128), 0), iota((512, 128), 1)
    hit = (at // 128 == lane // 32) & (at % 128 // 4 == lane % 32)
    gather[...] = jnp.where(hit, 1.0 / 64, 0.0).astype(BF16)
    for h in range(2):
        halves[h].wait()
        own = 2 + 4 * h
        sums[h] = (cells[own] + cells[own + 1]) + (cells[own + 2] + cells[own + 3])
    parts = []
    for h in range(2):
        for half in range(2):
            parts.append(sum(sums[h, pl.ds(4 * half + j, 16, stride=8), :] for j in range(4)))
    wide = jnp.concatenate(split3(jnp.concatenate(parts, axis=1)), axis=0)
    means = jnp.dot(wide, gather[...], preferred_element_type=F32)
    window[REACH, 0] = means[:16] + means[16:32] + means[32:]

    fifteen = pltpu.make_async_remote_copy(
        lines.at[pl.ds(0, 15)], window.at[REACH, 1, pl.ds(0, 15)], line_send, line_recv,
        device_id=(s, (g + 1) % 16), device_id_type=MESH,
    )
    fifteen.wait_recv()
    near = []
    for k in range(1, REACH + 1):
        for i, o in ((2 * k - 2, k), (2 * k - 1, -k)):
            copy = pltpu.make_async_remote_copy(
                window.at[REACH], window.at[REACH - o], near_send.at[i], near_recv.at[i],
                device_id=device(me + o), device_id_type=MESH,
            )
            goes = (me + o >= 0) & (me + o < pairs)
            comes = (me - o >= 0) & (me - o < pairs)
            pl.when(goes)(copy.start)
            near.append((copy, goes, comes))

    halo = []
    for i, (o, src, dst) in enumerate(((1, comp.at[6:8], cells.at[0:2]), (-1, comp.at[0:2], cells.at[10:12]))):
        copy = pltpu.make_async_remote_copy(
            src, dst, halo_send.at[i], halo_recv.at[i], device_id=device(me + o), device_id_type=MESH
        )
        goes = (me + o >= 0) & (me + o < pairs)
        comes = (me - o >= 0) & (me - o < pairs)
        pl.when(goes)(copy.start)
        halo.append((copy, goes, comes))

    at, lane = iota((128, 512), 0), iota((128, 512), 1)
    hit = (lane // 128 == at // 32) & (lane % 128 // 4 == at % 32)
    z_mat[0] = jnp.where(hit, 1.0, 0.0).astype(BF16)
    z_mat[1] = jnp.where(hit & (lane % 4 == 0), 1.0, 0.0).astype(BF16)
    z_mat[2] = jnp.where(hit & (lane % 4 == 3), 1.0, 0.0).astype(BF16)
    at, lane = iota((128, 192), 0), iota((128, 192), 1)
    coarse = 2 * (lane % 16) + (lane // 16) % 2
    same, second = spread(at, coarse)
    y_mat[...] = jnp.where(lane < 96, second, same).astype(BF16)

    def chemical(p):
        u = cells[p + 2]
        around = cells[p + 1] + cells[p + 3] + plane_neighbours(u)
        chem[p + 1] = u * u * u + 2.0 * u - 0.5 * around

    def partial(f):
        mu = chem[f + 1]
        around = chem[f] + chem[f + 2] + plane_neighbours(mu)
        out[f] = cells[f + 2] + 0.02 * (around - 6.0 * mu)

    lax.fori_loop(1, 7, lambda p, _: (chemical(p), 0)[1], 0)
    lax.fori_loop(2, 6, lambda f, _: (partial(f), 0)[1], 0)

    for copy, goes, comes in near:
        pl.when(comes)(copy.wait_recv)
    potential = coarse_cycle(
        window[:, 0].reshape(WINDOW * 16, 128), window[:, 1].reshape(WINDOW * 16, 128), me - REACH, pairs
    )
    centre = potential[16:32]
    lines_p = potline
    lines_p[...] = centre
    for k in range(1, 16):
        to = (g + k) % 16
        pltpu.make_async_remote_copy(
            lines_p.at[pl.ds(to, 1)], pot.at[pl.ds(g, 1)], pot_send, pot_recv,
            device_id=(s, to), device_id_type=MESH,
        ).start()
    pot[pl.ds(g, 1), :] = lines_p[pl.ds(g, 1), :]

    lane = iota((16, 128), 1)
    swapped = pltpu.roll(potential, 64, 1)
    before = jnp.where(lane < 64, swapped[:16], swapped[16:32]) - centre
    after = jnp.where(lane < 64, swapped[16:32], swapped[32:]) - centre
    left = jnp.where(lane % 32 > 0, lanes(centre, -1), 0.0) - centre
    right = jnp.where(lane % 32 < 31, lanes(centre, 1), 0.0) - centre
    t0 = jnp.dot(
        jnp.concatenate(split3(centre) + split3(before) + split3(after), 0), z_mat[0],
        preferred_element_type=F32,
    ).astype(BF16)
    t1 = jnp.dot(
        jnp.concatenate([jnp.concatenate(split3(left), 0), jnp.concatenate(split3(right), 0)], 1),
        z_mat[1:].reshape(256, 512), preferred_element_type=F32,
    ).astype(BF16)

    def stacked(t, at, column):
        return [
            t[at + 16 * i : at + 16 * i + 16, column + 128 * py : column + 128 * py + 128]
            for i in range(3)
            for py in range(2)
        ]

    for copy, goes, comes in halo:
        pl.when(comes)(copy.wait_recv)
    zero = jnp.zeros((2, 128, 128), F32)

    @pl.when(me == 0)
    def _():
        cells[0:2] = zero

    @pl.when(me == pairs - 1)
    def _():
        cells[10:12] = zero

    for p in (-1, 0, 7, 8):
        chemical(p)

    @pl.when(me == 0)
    def _():
        chem[0] = zero[0]

    @pl.when(me == pairs - 1)
    def _():
        chem[9] = zero[0]

    for f in (0, 1, 6, 7):
        partial(f)

    for px in range(2):
        rhs = jnp.concatenate(stacked(t0, 0, 256 * px) + stacked(t1, 0, 256 * px), 0)
        base = 0.08 * jnp.dot(y_mat[...], rhs, preferred_element_type=F32)
        low = 0.08 * jnp.dot(
            y_mat[:, 96:], jnp.concatenate(stacked(t0, 48, 256 * px), 0), preferred_element_type=F32
        )
        high = 0.08 * jnp.dot(
            y_mat[:, 96:], jnp.concatenate(stacked(t0, 96, 256 * px), 0), preferred_element_type=F32
        )
        out[4 * px] += base + low
        out[4 * px + 1] += base
        out[4 * px + 2] += base
        out[4 * px + 3] += base + high

    done = pltpu.make_async_remote_copy(
        lines_p.at[pl.ds(0, 15)], pot.at[pl.ds(0, 15)], pot_send, pot_recv,
        device_id=(s, (g + 1) % 16), device_id_type=MESH,
    )
    done.wait_recv()
    fifteen.wait_send()
    done.wait_send()
    for copy, goes, comes in near + halo:
        pl.when(goes)(copy.wait_send)


def unpack(fine, lines, out, pot, sem):
    copy = pltpu.make_async_copy(fine, out, sem)
    copy.start()
    packed = pot.reshape(64, 32)
    for k in range(4):
        packed[pl.ds(k, 16, stride=4), :] = lines[:, 32 * k : 32 * k + 32]
    copy.wait()


def per_device(comp, guess):
    slabs = lax.axis_size("slab")
    dma = pltpu.SemaphoreType.DMA

    def body(*refs):
        step(slabs, *refs)

    vmem = pl.BlockSpec(memory_space=pltpu.VMEM)
    anywhere = pl.BlockSpec(memory_space=pl.ANY)
    fine, lines = pl.pallas_call(
        body,
        out_shape=(jax.ShapeDtypeStruct((8, 128, 128), F32), jax.ShapeDtypeStruct((16, 128), F32)),
        in_specs=[pl.BlockSpec(memory_space=pltpu.HBM)] * 2,
        out_specs=(vmem, vmem),
        scratch_shapes=[
            pltpu.VMEM((12, 128, 128), F32),
            pltpu.VMEM((32, 2, 32), F32),
            pltpu.VMEM((16, 128), F32),
            pltpu.VMEM((WINDOW, 2, 16, 128), F32),
            pltpu.VMEM((10, 128, 128), F32),
            pltpu.VMEM((2, 128, 128), F32),
            pltpu.VMEM((512, 128), BF16),
            pltpu.VMEM((3, 128, 512), BF16),
            pltpu.VMEM((128, 192), BF16),
            pltpu.VMEM((16, 128), F32),
            dma((2,)),
            dma,
            dma,
            dma,
            dma((2 * REACH,)),
            dma((2 * REACH,)),
            dma((2,)),
            dma((2,)),
            dma,
            dma,
        ],
        compiler_params=pltpu.CompilerParams(
            collective_id=0, has_side_effects=True, vmem_limit_bytes=32 * 1024 * 1024
        ),
        name="step",
    )(comp, guess)
    return pl.pallas_call(
        unpack,
        out_shape=(jax.ShapeDtypeStruct(comp.shape, F32), jax.ShapeDtypeStruct(guess.shape, F32)),
        in_specs=[vmem, vmem],
        out_specs=(pl.BlockSpec(memory_space=pltpu.HBM), vmem),
        scratch_shapes=[dma],
        name="unpack",
    )(fine, lines)


def solution(mesh):
    placed = (P(("slab", "grp"), None, None), P("slab", "grp", None))
    return jax.shard_map(
        per_device, mesh=mesh, in_specs=placed, out_specs=placed, check_vma=False
    )
```

time: 159 us -> 36 us (0.23)
  local copies, waits for them, and re-layouts: 65.3 us -> 3.18 us
  blocking collectives: 35 us -> 0 us
  starting transfers between devices: 32.1 us -> 0 us
  Pallas kernels: 0 us -> 32 us
  other arithmetic: 17.9 us -> 0 us
  waiting for transfers between devices: 7.25 us -> 0 us
    reshape x5 -> x0, local copies, waits for them, and re-layouts: 35 us -> none  [the longest x2 27.5 us: block_mean(): field.reshape(first // factor, factor, second // factor, factor, third //...]
    all_gather x1 -> x0, blocking collectives: 35 us -> none  [gather_together(): lines, at, done = (lax.all_gather(ravelled, axis), 0, [])]
    ppermute x8 -> x0, starting transfers between devices: 32.1 us -> none  [the longest x2 14.5 us: extended_2(): lax.ppermute(lax.slice_in_dim(block, 0, width, axis=dim), axis, backward)]
    pallas_call x0 -> x2, Pallas kernels: none -> 32 us  [the longest x1 29.5 us: per_device(): pl.pallas_call(body, out_shape=(jax.ShapeDtypeStruct((8, 128, 128), F32),...]
    mul x1 -> x0, local copies, waits for them, and re-layouts: 14.8 us -> none  [per_device(): field = chem + long_range * expand(slab_planes, 4)]
    broadcast_in_dim x2 -> x0, local copies, waits for them, and re-layouts: 12.3 us -> none  [expand(): jnp.broadcast_to(field[:, None, :, None, :, None], (first, factor, second...]
    reduce_sum x2 -> x0, other arithmetic: 12.2 us -> none  [block_mean(): return field.reshape(first // factor, factor, second // factor, factor, t...]
    ppermute x8 -> x0, waiting for transfers between devices: 7.25 us -> none  [the longest x2 7.23 us: padded_2(): lax.ppermute(last, axis, up)]
  transfers between devices with their start and end apart: 8 -> 0, of which waited for: 1 -> 0; matrix products, arithmetic and copies ran while one was open for 34% -> 0% of each run, Pallas kernels for 0% -> 0%
where the time goes in v1:
time: 36 us; the launch traced here: 35.8 us
  Pallas kernels  32 us (89%)
  local copies, waits for them, and re-layouts  3.18 us (9%)
  between operations  0.66 us (2%)
    pallas_call x1, Pallas kernels, per_device(): pl.pallas_call(body, out_shape=(jax.ShapeDtypeStruct((8, 128, 128), F32),...  29.5 us
    unnamed x8, local copies, waits for them, and re-layouts  3.18 us
    pallas_call x1, Pallas kernels, per_device(): pl.pallas_call(unpack, out_shape=(jax.ShapeDtypeStruct(comp.shape, F32),...  2.46 us

profile of v1, /device:TPU:4, one launch (start us, length us, event | category | flops | bytes accessed | tf_op | source)
XLA Modules:
  0.0 35.8 jit_solution(9380204978170973934)
XLA Ops:
  0.6 0.0 copy-start
  0.6 1.0 %copy-done = f32[8,128,128]{2,1,0:T(8,128)S(1)} copy-done((f32[8,128,128]{2,1,0:T(8,128)S(1)}, f32[8,128,128]{2,1,0:T(8,128)}, u32[]{:S(2)}) %copy-start) | copy-done | bytes 524312
  1.7 0.0 copy-start.2
  1.7 0.8 %copy-done.2 = f32[32,2,32]{2,1,0:T(2,128)S(1)} copy-done((f32[32,2,32]{2,1,0:T(2,128)S(1)}, f32[32,2,32]{2,1,0:T(2,128)}, u32[]{:S(2)}) %copy-start.2) | copy-done | bytes 8216
  2.4 29.5 %step.1 = (f32[8,128,128]{2,1,0:T(8,128)S(1)}, f32[16,128]{1,0:T(8,128)S(1)}) custom-call(f32[8,128,128]{2,1,0:T(8,128)S(1)} %copy-done, f32[32,2,32]{2,1,0:T(2,128)S(1)} %copy-done.2), custom_call_target="tpu_custom_call" | custom-call | tf_op jit(solution)/shard_map/step/pallas_call | solution.py:319
  31.9 0.0 copy-start.1
  31.9 0.8 %copy-done.1 = f32[8,128,128]{2,1,0:T(8,128)} copy-done((f32[8,128,128]{2,1,0:T(8,128)}, f32[8,128,128]{2,1,0:T(8,128)S(1)}, u32[]{:S(2)}) %copy-start.1) | copy-done | bytes 524312
  32.7 0.0 copy-start.3
  32.7 0.6 %copy-done.3 = f32[16,128]{1,0:T(8,128)} copy-done((f32[16,128]{1,0:T(8,128)}, f32[16,128]{1,0:T(8,128)S(1)}, u32[]{:S(2)}) %copy-start.3) | copy-done | bytes 8216
  33.3 2.5 %unpack.1 = (f32[8,128,128]{2,1,0:T(8,128)}, f32[32,2,32]{2,1,0:T(2,128)}) custom-call(f32[8,128,128]{2,1,0:T(8,128)} %copy-done.1, f32[16,128]{1,0:T(8,128)} %copy-done.3), custom_call_target="tpu_custom_call" | custom-call | tf_op jit(solution)/shard_map/unpack/pallas_call | solution.py:351
Async XLA Ops:
  0.6 1.0 %copy-start = (f32[8,128,128]{2,1,0:T(8,128)S(1)}, f32[8,128,128]{2,1,0:T(8,128)}, u32[]{:S(2)}) copy-start(f32[8,128,128]{2,1,0:T(8,128)} %refs_0_.1) | copy-start | bytes 1572868
  1.7 0.8 %copy-start.2 = (f32[32,2,32]{2,1,0:T(2,128)S(1)}, f32[32,2,32]{2,1,0:T(2,128)}, u32[]{:S(2)}) copy-start(f32[32,2,32]{2,1,0:T(2,128)} %refs_1_.1) | copy-start | bytes 24580
  31.9 0.8 %copy-start.1 = (f32[8,128,128]{2,1,0:T(8,128)}, f32[8,128,128]{2,1,0:T(8,128)S(1)}, u32[]{:S(2)}) copy-start(f32[8,128,128]{2,1,0:T(8,128)S(1)} %get-tuple-element.4.fine) | copy-start | bytes 1572868
  32.7 0.6 %copy-start.3 = (f32[16,128]{1,0:T(8,128)}, f32[16,128]{1,0:T(8,128)S(1)}, u32[]{:S(2)}) copy-start(f32[16,128]{1,0:T(8,128)S(1)} %get-tuple-element.5.lines) | copy-start | bytes 24580

commit v2 on v1

--- a/solution.py
+++ b/solution.py
@@ -8,6 +8,7 @@
 MESH = pl.DeviceIdType.MESH
 REACH = 5
 WINDOW = 2 * REACH + 1
+FAR_FIRST = (8, 7, 9, 6, 10, 5, 11, 4, 12, 3, 13, 2, 14, 1, 15)
 F32 = jnp.float32
 BF16 = jnp.bfloat16
 
@@ -97,13 +98,15 @@
 
 
 def step(
-    slabs, comp, guess, out, pot, cells, given, lines, window, chem, sums, gather, z_mat, y_mat,
-    potline, cell_sem, given_sem, line_send, line_recv, near_send, near_recv, halo_send,
-    halo_recv, pot_send, pot_recv,
+    slabs, comp, guess, out, pot, cells, given, lines, sources, guesses, beyond, chem, sums, gather, z_mat,
+    y_mat, centre, cell_sem, given_sem, line_send, line_recv, cross_send, cross_recv, near_send, near_recv,
+    halo_send, halo_recv, pot_send, pot_recv,
 ):
     s, g = lax.axis_index("slab"), lax.axis_index("grp")
     me = s * 16 + g
     pairs = slabs * 16
+    below, above = s > 0, s < slabs - 1
+    from_below, from_above = below & (g < REACH), above & (g >= 16 - REACH)
 
     def device(d):
         return (d // 16, d % 16)
@@ -118,31 +121,23 @@
         half.start()
 
     barrier = pltpu.get_barrier_semaphore()
-    crossing = jnp.int32(15)
-    for k in range(1, REACH + 1):
-        for d, across in ((me + k, g + k > 15), (me - k, g - k < 0)):
-            other = across & (d >= 0) & (d < pairs)
-            crossing += other.astype(jnp.int32)
-
-            @pl.when(other)
-            def _():
-                pl.semaphore_signal(barrier, 1, device_id=device(d), device_id_type=MESH)
-
-    for k in range(1, 16):
+    for there, other in ((from_below, s - 1), (from_above, s + 1)):
+
+        @pl.when(there)
+        def _():
+            for k in range(16):
+                pl.semaphore_signal(barrier, 1, device_id=(other, (g + k) % 16), device_id_type=MESH)
+
+    for k in FAR_FIRST:
         pl.semaphore_signal(barrier, 1, device_id=(s, (g + k) % 16), device_id_type=MESH)
 
     load_guess.wait()
     packed = given.reshape(64, 32)
-    lines[...] = jnp.concatenate([packed[pl.ds(k, 16, stride=4), :] for k in range(4)], axis=1)
-
-    pl.semaphore_wait(barrier, crossing)
-    for k in range(1, 16):
-        to = (g + k) % 16
-        pltpu.make_async_remote_copy(
-            lines.at[pl.ds(to, 1)], window.at[REACH, 1, pl.ds(g, 1)], line_send, line_recv,
-            device_id=(s, to), device_id_type=MESH,
-        ).start()
-    window[REACH, 1, pl.ds(g, 1), :] = lines[pl.ds(g, 1), :]
+    lines[0:REACH] = jnp.zeros((REACH, 128), F32)
+    lines[REACH + 16 :] = jnp.zeros((REACH, 128), F32)
+    lines[REACH : REACH + 16] = jnp.concatenate(
+        [packed[pl.ds(k, 16, stride=4), :] for k in range(4)], axis=1
+    )
 
     at, lane = iota((512, 128), 0), iota((512, 128), 1)
     hit = (at // 128 == lane // 32) & (at % 128 // 4 == lane % 32)
@@ -157,18 +152,41 @@
             parts.append(sum(sums[h, pl.ds(4 * half + j, 16, stride=8), :] for j in range(4)))
     wide = jnp.concatenate(split3(jnp.concatenate(parts, axis=1)), axis=0)
     means = jnp.dot(wide, gather[...], preferred_element_type=F32)
-    window[REACH, 0] = means[:16] + means[16:32] + means[32:]
-
-    fifteen = pltpu.make_async_remote_copy(
-        lines.at[pl.ds(0, 15)], window.at[REACH, 1, pl.ds(0, 15)], line_send, line_recv,
-        device_id=(s, (g + 1) % 16), device_id_type=MESH,
-    )
-    fifteen.wait_recv()
+    sources[REACH] = means[:16] + means[16:32] + means[32:]
+
+    pl.semaphore_wait(
+        barrier, 15 + REACH * (below.astype(jnp.int32) + above.astype(jnp.int32))
+    )
+
+    @pl.when(above)
+    def _():
+        for to in range(REACH):
+            pltpu.make_async_remote_copy(
+                lines.at[16 + to : 21], beyond.at[0 : REACH - to, g], cross_send.at[0], cross_recv,
+                device_id=(s + 1, to), device_id_type=MESH,
+            ).start()
+
+    @pl.when(below)
+    def _():
+        for to in range(16 - REACH, 16):
+            pltpu.make_async_remote_copy(
+                lines.at[REACH : to - 5], beyond.at[21 - to : WINDOW, g], cross_send.at[1], cross_recv,
+                device_id=(s - 1, to), device_id_type=MESH,
+            ).start()
+
+    for k in FAR_FIRST:
+        to = (g + k) % 16
+        pltpu.make_async_remote_copy(
+            lines.at[pl.ds(to, WINDOW)], guesses.at[:, g], line_send, line_recv,
+            device_id=(s, to), device_id_type=MESH,
+        ).start()
+    guesses[:, pl.ds(g, 1), :] = lines[pl.ds(g, WINDOW), :].reshape(WINDOW, 1, 128)
+
     near = []
-    for k in range(1, REACH + 1):
+    for k in range(REACH, 0, -1):
         for i, o in ((2 * k - 2, k), (2 * k - 1, -k)):
             copy = pltpu.make_async_remote_copy(
-                window.at[REACH], window.at[REACH - o], near_send.at[i], near_recv.at[i],
+                sources.at[REACH], sources.at[REACH - o], near_send.at[i], near_recv.at[i],
                 device_id=device(me + o), device_id_type=MESH,
             )
             goes = (me + o >= 0) & (me + o < pairs)
@@ -209,30 +227,49 @@
     lax.fori_loop(1, 7, lambda p, _: (chemical(p), 0)[1], 0)
     lax.fori_loop(2, 6, lambda f, _: (partial(f), 0)[1], 0)
 
+    lines_in = pltpu.make_async_remote_copy(
+        guesses.at[:, 0:15], guesses.at[:, 0:15], line_send, line_recv,
+        device_id=(s, (g + 1) % 16), device_id_type=MESH,
+    )
+    lines_in.wait_recv()
+    for there, spots in (
+        (from_below, [(j, slice(0, REACH - j)) for j in range(REACH)]),
+        (from_above, [(j, slice(21 - j, WINDOW)) for j in range(16 - REACH, 16)]),
+    ):
+        for j, spot in spots:
+
+            @pl.when(there & (g == j))
+            def _():
+                pltpu.make_async_remote_copy(
+                    beyond.at[spot], beyond.at[spot], cross_send.at[0], cross_recv,
+                    device_id=(s, (g + 1) % 16), device_id_type=MESH,
+                ).wait_recv()
+
     for copy, goes, comes in near:
         pl.when(comes)(copy.wait_recv)
-    potential = coarse_cycle(
-        window[:, 0].reshape(WINDOW * 16, 128), window[:, 1].reshape(WINDOW * 16, 128), me - REACH, pairs
-    )
-    centre = potential[16:32]
-    lines_p = potline
-    lines_p[...] = centre
-    for k in range(1, 16):
+    place = g - REACH + iota((WINDOW * 16, 128), 0) // 16
+    start = jnp.where(
+        (place >= 0) & (place < 16), guesses[...].reshape(WINDOW * 16, 128), beyond[...].reshape(WINDOW * 16, 128)
+    )
+    potential = coarse_cycle(sources[...].reshape(WINDOW * 16, 128), start, me - REACH, pairs)
+    own = potential[16:32]
+    centre[...] = own
+    for k in FAR_FIRST:
         to = (g + k) % 16
         pltpu.make_async_remote_copy(
-            lines_p.at[pl.ds(to, 1)], pot.at[pl.ds(g, 1)], pot_send, pot_recv,
+            centre.at[pl.ds(to, 1)], pot.at[pl.ds(g, 1)], pot_send, pot_recv,
             device_id=(s, to), device_id_type=MESH,
         ).start()
-    pot[pl.ds(g, 1), :] = lines_p[pl.ds(g, 1), :]
+    pot[pl.ds(g, 1), :] = centre[pl.ds(g, 1), :]
 
     lane = iota((16, 128), 1)
     swapped = pltpu.roll(potential, 64, 1)
-    before = jnp.where(lane < 64, swapped[:16], swapped[16:32]) - centre
-    after = jnp.where(lane < 64, swapped[16:32], swapped[32:]) - centre
-    left = jnp.where(lane % 32 > 0, lanes(centre, -1), 0.0) - centre
-    right = jnp.where(lane % 32 < 31, lanes(centre, 1), 0.0) - centre
+    before = jnp.where(lane < 64, swapped[:16], swapped[16:32]) - own
+    after = jnp.where(lane < 64, swapped[16:32], swapped[32:]) - own
+    left = jnp.where(lane % 32 > 0, lanes(own, -1), 0.0) - own
+    right = jnp.where(lane % 32 < 31, lanes(own, 1), 0.0) - own
     t0 = jnp.dot(
-        jnp.concatenate(split3(centre) + split3(before) + split3(after), 0), z_mat[0],
+        jnp.concatenate(split3(own) + split3(before) + split3(after), 0), z_mat[0],
         preferred_element_type=F32,
     ).astype(BF16)
     t1 = jnp.dot(
@@ -288,12 +325,21 @@
         out[4 * px + 3] += base + high
 
     done = pltpu.make_async_remote_copy(
-        lines_p.at[pl.ds(0, 15)], pot.at[pl.ds(0, 15)], pot_send, pot_recv,
+        centre.at[pl.ds(0, 15)], pot.at[pl.ds(0, 15)], pot_send, pot_recv,
         device_id=(s, (g + 1) % 16), device_id_type=MESH,
     )
     done.wait_recv()
-    fifteen.wait_send()
     done.wait_send()
+    lines_in.wait_send()
+    for i, there in ((0, above), (1, below)):
+
+        @pl.when(there)
+        def _():
+            pltpu.make_async_remote_copy(
+                lines.at[0:15], lines.at[0:15], cross_send.at[i], cross_recv,
+                device_id=(s, (g + 1) % 16), device_id_type=MESH,
+            ).wait_send()
+
     for copy, goes, comes in near + halo:
         pl.when(goes)(copy.wait_send)
 
@@ -318,14 +364,16 @@
     anywhere = pl.BlockSpec(memory_space=pl.ANY)
     fine, lines = pl.pallas_call(
         body,
-        out_shape=(jax.ShapeDtypeStruct((8, 128, 128), F32), jax.ShapeDtypeStruct((16, 128), F32)),
+        out_shape=(pltpu.VMEM((8, 128, 128), F32), pltpu.VMEM((16, 128), F32)),
         in_specs=[pl.BlockSpec(memory_space=pltpu.HBM)] * 2,
         out_specs=(vmem, vmem),
         scratch_shapes=[
             pltpu.VMEM((12, 128, 128), F32),
             pltpu.VMEM((32, 2, 32), F32),
-            pltpu.VMEM((16, 128), F32),
-            pltpu.VMEM((WINDOW, 2, 16, 128), F32),
+            pltpu.VMEM((16 + 2 * REACH, 128), F32),
+            pltpu.VMEM((WINDOW, 16, 128), F32),
+            pltpu.VMEM((WINDOW, 16, 128), F32),
+            pltpu.VMEM((WINDOW, 16, 128), F32),
             pltpu.VMEM((10, 128, 128), F32),
             pltpu.VMEM((2, 128, 128), F32),
             pltpu.VMEM((512, 128), BF16),
@@ -336,6 +384,8 @@
             dma,
             dma,
             dma,
+            dma((2,)),
+            dma,
             dma((2 * REACH,)),
             dma((2 * REACH,)),
             dma((2,)),
@@ -344,7 +394,7 @@
             dma,
         ],
         compiler_params=pltpu.CompilerParams(
-            collective_id=0, has_side_effects=True, vmem_limit_bytes=32 * 1024 * 1024
+            collective_id=0, has_side_effects=True, vmem_limit_bytes=62 * 1024 * 1024
         ),
         name="step",
     )(comp, guess)
@@ -354,6 +404,7 @@
         in_specs=[vmem, vmem],
         out_specs=(pl.BlockSpec(memory_space=pltpu.HBM), vmem),
         scratch_shapes=[dma],
+        compiler_params=pltpu.CompilerParams(vmem_limit_bytes=1024 * 1024),
         name="unpack",
     )(fine, lines)
 

time: 36 us -> 29.1 us (0.81)
  the two profiles are of different devices: /device:TPU:4 before, /device:TPU:6 now
where the time goes in v2:
time: 29.1 us; the launch traced here: 29 us
  Pallas kernels  28.4 us (98%)
  between operations  0.64 us (2%)
    pallas_call x1, Pallas kernels, per_device(): pl.pallas_call(body, out_shape=(pltpu.VMEM((8, 128, 128), F32), pltpu.VME...  26.9 us
    pallas_call x1, Pallas kernels, per_device(): pl.pallas_call(unpack, out_shape=(jax.ShapeDtypeStruct(comp.shape, F32),...  1.42 us

profile of v2, /device:TPU:6, one launch (start us, length us, event | category | flops | bytes accessed | tf_op | source)
XLA Modules:
  0.0 29.0 jit_solution(4766156801517702426)
XLA Ops:
  0.6 26.9 %step.1 = (f32[8,128,128]{2,1,0:T(8,128)S(1)}, f32[16,128]{1,0:T(8,128)S(1)}) custom-call(f32[8,128,128]{2,1,0:T(8,128)} %refs_0_.1, f32[32,2,32]{2,1,0:T(2,128)} %refs_1_.1), custom_call_target="tpu_custom_call" | custom-call | tf_op jit(solution)/shard_map/step/pallas_call | solution.py:365
  27.6 1.4 %unpack.1 = (f32[8,128,128]{2,1,0:T(8,128)}, f32[32,2,32]{2,1,0:T(2,128)}) custom-call(f32[8,128,128]{2,1,0:T(8,128)S(1)} %get-tuple-element.4.fine, f32[16,128]{1,0:T(8,128)S(1)} %get-tuple-element.5.lines), custom_call_target="tpu_custom_call" | custom-call | tf_op jit(solution)/shard_map/unpack/pallas_call | solution.py:401

commit v3 on v2

--- a/solution.py
+++ b/solution.py
@@ -8,6 +8,7 @@
 MESH = pl.DeviceIdType.MESH
 REACH = 5
 WINDOW = 2 * REACH + 1
+HUB = 8
 FAR_FIRST = (8, 7, 9, 6, 10, 5, 11, 4, 12, 3, 13, 2, 14, 1, 15)
 F32 = jnp.float32
 BF16 = jnp.bfloat16
@@ -98,15 +99,17 @@
 
 
 def step(
-    slabs, comp, guess, out, pot, cells, given, lines, sources, guesses, beyond, chem, sums, gather, z_mat,
-    y_mat, centre, cell_sem, given_sem, line_send, line_recv, cross_send, cross_recv, near_send, near_recv,
-    halo_send, halo_recv, pot_send, pot_recv,
+    slabs, comp, guess, out, result, cells, given, lines, sources, guesses, beyond, chem, sums, gather, z_mat,
+    y_mat, centre, pot, cell_sem, given_sem, line_send, line_recv, cross_send, cross_recv, near_send, near_recv,
+    halo_send, halo_recv, pot_send, pot_recv, word,
 ):
     s, g = lax.axis_index("slab"), lax.axis_index("grp")
     me = s * 16 + g
     pairs = slabs * 16
     below, above = s > 0, s < slabs - 1
     from_below, from_above = below & (g < REACH), above & (g >= 16 - REACH)
+    middle = slabs // 2
+    late, early, hub = s == middle - 1, s == middle, (s == middle - 2) & (g == HUB)
 
     def device(d):
         return (d // 16, d % 16)
@@ -121,15 +124,28 @@
         half.start()
 
     barrier = pltpu.get_barrier_semaphore()
-    for there, other in ((from_below, s - 1), (from_above, s + 1)):
-
-        @pl.when(there)
+    across = from_below | (from_above & (s != middle - 1) & (s != middle - 2))
+    other = jnp.where(g < REACH, s - 1, s + 1)
+    for k in FAR_FIRST + (0,):
+        peer = (g + k) % 16
+        if k:
+
+            @pl.when(jnp.logical_not(late))
+            def _():
+                pl.semaphore_signal(barrier, 1, device_id=(s, peer), device_id_type=MESH)
+
+        @pl.when(across)
         def _():
-            for k in range(16):
-                pl.semaphore_signal(barrier, 1, device_id=(other, (g + k) % 16), device_id_type=MESH)
-
-    for k in FAR_FIRST:
-        pl.semaphore_signal(barrier, 1, device_id=(s, (g + k) % 16), device_id_type=MESH)
+            pl.semaphore_signal(barrier, 1, device_id=(other, peer), device_id_type=MESH)
+
+    @pl.when(late)
+    def _():
+        pl.semaphore_signal(barrier, 1, device_id=(s - 1, HUB), device_id_type=MESH)
+
+    @pl.when(early & (g >= REACH))
+    def _():
+        for to in range(16 - REACH, 16):
+            pl.semaphore_signal(barrier, 1, device_id=(s - 1, to), device_id_type=MESH)
 
     load_guess.wait()
     packed = given.reshape(64, 32)
@@ -138,6 +154,25 @@
     lines[REACH : REACH + 16] = jnp.concatenate(
         [packed[pl.ds(k, 16, stride=4), :] for k in range(4)], axis=1
     )
+
+    def guess_up():
+        for to in range(REACH):
+            pltpu.make_async_remote_copy(
+                lines.at[16 + to : 21], beyond.at[0 : REACH - to, g], cross_send.at[0], cross_recv,
+                device_id=(s + 1, to), device_id_type=MESH,
+            ).start()
+
+    @pl.when(late)
+    def _():
+        pl.semaphore_wait(barrier, jnp.where(g < 16 - REACH, REACH, 16))
+        guess_up()
+
+        @pl.when(g >= 16 - REACH)
+        def _():
+            for k in range(16):
+                pl.semaphore_signal(
+                    word.at[0], 1, device_id=(s + 1, (g + k) % 16), device_id_type=MESH
+                )
 
     at, lane = iota((512, 128), 0), iota((512, 128), 1)
     hit = (at // 128 == lane // 32) & (at % 128 // 4 == lane % 32)
@@ -154,26 +189,54 @@
     means = jnp.dot(wide, gather[...], preferred_element_type=F32)
     sources[REACH] = means[:16] + means[16:32] + means[32:]
 
-    pl.semaphore_wait(
-        barrier, 15 + REACH * (below.astype(jnp.int32) + above.astype(jnp.int32))
-    )
-
-    @pl.when(above)
-    def _():
-        for to in range(REACH):
-            pltpu.make_async_remote_copy(
-                lines.at[16 + to : 21], beyond.at[0 : REACH - to, g], cross_send.at[0], cross_recv,
-                device_id=(s + 1, to), device_id_type=MESH,
-            ).start()
-
-    @pl.when(below)
-    def _():
+    @pl.when(jnp.logical_not(late))
+    def _():
+        asked = REACH * (above.astype(jnp.int32) + (below & jnp.logical_not(early)).astype(jnp.int32))
+        pl.semaphore_wait(barrier, 15 + asked + 16 * hub.astype(jnp.int32))
+
+    @pl.when(hub)
+    def _():
+        for to in range(16):
+            pl.semaphore_signal(word.at[1], 1, device_id=(s + 1, to), device_id_type=MESH)
+
+    pl.when(above & jnp.logical_not(late))(guess_up)
+
+    near = []
+    for k in range(REACH, 0, -1):
+        for i, o in ((2 * k - 2, k), (2 * k - 1, -k)):
+            copy = pltpu.make_async_remote_copy(
+                sources.at[REACH], sources.at[REACH - o], near_send.at[i], near_recv.at[i],
+                device_id=device(me + o), device_id_type=MESH,
+            )
+            near.append((copy, o))
+    halo = []
+    for i, (o, src, dst) in enumerate(((1, comp.at[6:8], cells.at[0:2]), (-1, comp.at[0:2], cells.at[10:12]))):
+        copy = pltpu.make_async_remote_copy(
+            src, dst, halo_send.at[i], halo_recv.at[i], device_id=device(me + o), device_id_type=MESH
+        )
+        halo.append((copy, o))
+
+    def goes(o):
+        return (me + o >= 0) & (me + o < pairs)
+
+    def comes(o):
+        return (me - o >= 0) & (me - o < pairs)
+
+    def guess_down():
         for to in range(16 - REACH, 16):
             pltpu.make_async_remote_copy(
                 lines.at[REACH : to - 5], beyond.at[21 - to : WINDOW, g], cross_send.at[1], cross_recv,
                 device_id=(s - 1, to), device_id_type=MESH,
             ).start()
 
+    @pl.when(late)
+    def _():
+        for copy, o in near + halo:
+            if o > 0:
+                pl.when(g + o > 15)(copy.start)
+        pl.semaphore_wait(word.at[1], 1)
+
+    pl.when(below & jnp.logical_not(early))(guess_down)
     for k in FAR_FIRST:
         to = (g + k) % 16
         pltpu.make_async_remote_copy(
@@ -181,28 +244,18 @@
             device_id=(s, to), device_id_type=MESH,
         ).start()
     guesses[:, pl.ds(g, 1), :] = lines[pl.ds(g, WINDOW), :].reshape(WINDOW, 1, 128)
-
-    near = []
-    for k in range(REACH, 0, -1):
-        for i, o in ((2 * k - 2, k), (2 * k - 1, -k)):
-            copy = pltpu.make_async_remote_copy(
-                sources.at[REACH], sources.at[REACH - o], near_send.at[i], near_recv.at[i],
-                device_id=device(me + o), device_id_type=MESH,
-            )
-            goes = (me + o >= 0) & (me + o < pairs)
-            comes = (me - o >= 0) & (me - o < pairs)
-            pl.when(goes)(copy.start)
-            near.append((copy, goes, comes))
-
-    halo = []
-    for i, (o, src, dst) in enumerate(((1, comp.at[6:8], cells.at[0:2]), (-1, comp.at[0:2], cells.at[10:12]))):
-        copy = pltpu.make_async_remote_copy(
-            src, dst, halo_send.at[i], halo_recv.at[i], device_id=device(me + o), device_id_type=MESH
-        )
-        goes = (me + o >= 0) & (me + o < pairs)
-        comes = (me - o >= 0) & (me - o < pairs)
-        pl.when(goes)(copy.start)
-        halo.append((copy, goes, comes))
+    for copy, o in near + halo:
+        inside = (g + o >= 0) & (g + o < 16)
+        rest = jnp.logical_not(late) if o > 0 else jnp.logical_not(early)
+        pl.when(inside | (goes(o) & rest))(copy.start)
+
+    @pl.when(early)
+    def _():
+        pl.semaphore_wait(word.at[0], REACH)
+        guess_down()
+        for copy, o in near + halo:
+            if o < 0:
+                pl.when(g + o < 0)(copy.start)
 
     at, lane = iota((128, 512), 0), iota((128, 512), 1)
     hit = (lane // 128 == at // 32) & (lane % 128 // 4 == at % 32)
@@ -245,8 +298,8 @@
                     device_id=(s, (g + 1) % 16), device_id_type=MESH,
                 ).wait_recv()
 
-    for copy, goes, comes in near:
-        pl.when(comes)(copy.wait_recv)
+    for copy, o in near:
+        pl.when(comes(o))(copy.wait_recv)
     place = g - REACH + iota((WINDOW * 16, 128), 0) // 16
     start = jnp.where(
         (place >= 0) & (place < 16), guesses[...].reshape(WINDOW * 16, 128), beyond[...].reshape(WINDOW * 16, 128)
@@ -284,8 +337,8 @@
             for py in range(2)
         ]
 
-    for copy, goes, comes in halo:
-        pl.when(comes)(copy.wait_recv)
+    for copy, o in halo:
+        pl.when(comes(o))(copy.wait_recv)
     zero = jnp.zeros((2, 128, 128), F32)
 
     @pl.when(me == 0)
@@ -329,6 +382,9 @@
         device_id=(s, (g + 1) % 16), device_id_type=MESH,
     )
     done.wait_recv()
+    packed = result.reshape(64, 32)
+    for k in range(4):
+        packed[pl.ds(k, 16, stride=4), :] = pot[:, 32 * k : 32 * k + 32]
     done.wait_send()
     lines_in.wait_send()
     for i, there in ((0, above), (1, below)):
@@ -340,17 +396,16 @@
                 device_id=(s, (g + 1) % 16), device_id_type=MESH,
             ).wait_send()
 
-    for copy, goes, comes in near + halo:
-        pl.when(goes)(copy.wait_send)
-
-
-def unpack(fine, lines, out, pot, sem):
-    copy = pltpu.make_async_copy(fine, out, sem)
-    copy.start()
-    packed = pot.reshape(64, 32)
-    for k in range(4):
-        packed[pl.ds(k, 16, stride=4), :] = lines[:, 32 * k : 32 * k + 32]
-    copy.wait()
+    for copy, o in near + halo:
+        pl.when(goes(o))(copy.wait_send)
+
+
+def deliver(fine, coarse, out, pot, sem):
+    copies = [pltpu.make_async_copy(fine, out, sem.at[0]), pltpu.make_async_copy(coarse, pot, sem.at[1])]
+    for copy in copies:
+        copy.start()
+    for copy in copies:
+        copy.wait()
 
 
 def per_device(comp, guess):
@@ -364,7 +419,7 @@
     anywhere = pl.BlockSpec(memory_space=pl.ANY)
     fine, lines = pl.pallas_call(
         body,
-        out_shape=(pltpu.VMEM((8, 128, 128), F32), pltpu.VMEM((16, 128), F32)),
+        out_shape=(pltpu.VMEM((8, 128, 128), F32), pltpu.VMEM((32, 2, 32), F32)),
         in_specs=[pl.BlockSpec(memory_space=pltpu.HBM)] * 2,
         out_specs=(vmem, vmem),
         scratch_shapes=[
@@ -380,6 +435,7 @@
             pltpu.VMEM((3, 128, 512), BF16),
             pltpu.VMEM((128, 192), BF16),
             pltpu.VMEM((16, 128), F32),
+            pltpu.VMEM((16, 128), F32),
             dma((2,)),
             dma,
             dma,
@@ -392,6 +448,7 @@
             dma((2,)),
             dma,
             dma,
+            pltpu.SemaphoreType.REGULAR((2,)),
         ],
         compiler_params=pltpu.CompilerParams(
             collective_id=0, has_side_effects=True, vmem_limit_bytes=62 * 1024 * 1024
@@ -399,13 +456,13 @@
         name="step",
     )(comp, guess)
     return pl.pallas_call(
-        unpack,
+        deliver,
         out_shape=(jax.ShapeDtypeStruct(comp.shape, F32), jax.ShapeDtypeStruct(guess.shape, F32)),
         in_specs=[vmem, vmem],
-        out_specs=(pl.BlockSpec(memory_space=pltpu.HBM), vmem),
-        scratch_shapes=[dma],
+        out_specs=(pl.BlockSpec(memory_space=pltpu.HBM),) * 2,
+        scratch_shapes=[dma((2,))],
         compiler_params=pltpu.CompilerParams(vmem_limit_bytes=1024 * 1024),
-        name="unpack",
+        name="deliver",
     )(fine, lines)
 
 

time: 29.1 us -> 24.3 us (0.84)
  the two profiles are of different devices: /device:TPU:6 before, /device:TPU:193 now
where the time goes in v3:
time: 24.3 us; the launch traced here: 24.2 us
  Pallas kernels  23.5 us (97%)
  between operations  0.64 us (3%)
    pallas_call x1, Pallas kernels, per_device(): pl.pallas_call(body, out_shape=(pltpu.VMEM((8, 128, 128), F32), pltpu.VME...  22.7 us
    pallas_call x1, Pallas kernels, per_device(): pl.pallas_call(deliver, out_shape=(jax.ShapeDtypeStruct(comp.shape, F32),...  0.81 us

profile of v3, /device:TPU:193, one launch (start us, length us, event | category | flops | bytes accessed | tf_op | source)
XLA Modules:
  0.0 24.2 jit_solution(16472858636010422412)
XLA Ops:
  0.6 22.7 %step.1 = (f32[8,128,128]{2,1,0:T(8,128)S(1)}, f32[32,2,32]{2,1,0:T(2,128)S(1)}) custom-call(f32[8,128,128]{2,1,0:T(8,128)} %refs_0_.1, f32[32,2,32]{2,1,0:T(2,128)} %refs_1_.1), custom_call_target="tpu_custom_call" | custom-call | tf_op jit(solution)/shard_map/step/pallas_call | solution.py:420
  23.4 0.8 %deliver.1 = (f32[8,128,128]{2,1,0:T(8,128)}, f32[32,2,32]{2,1,0:T(2,128)}) custom-call(f32[8,128,128]{2,1,0:T(8,128)S(1)} %get-tuple-element.4.fine, f32[32,2,32]{2,1,0:T(2,128)S(1)} %get-tuple-element.5.coarse), custom_call_target="tpu_custom_call" | custom-call | tf_op jit(solution)/shard_map/deliver/pallas_call | solution.py:458

commit v4 on v3

--- a/solution.py
+++ b/solution.py
@@ -7,7 +7,8 @@
 
 MESH = pl.DeviceIdType.MESH
 REACH = 5
-WINDOW = 2 * REACH + 1
+WINDOW = 2 * REACH + 2
+UPPER, LOWER = (0, 2, 4), (10, 12, 14)
 HUB = 8
 FAR_FIRST = (8, 7, 9, 6, 10, 5, 11, 4, 12, 3, 13, 2, 14, 1, 15)
 F32 = jnp.float32
@@ -100,19 +101,28 @@
 
 def step(
     slabs, comp, guess, out, result, cells, given, lines, sources, guesses, beyond, chem, sums, gather, z_mat,
-    y_mat, centre, pot, cell_sem, given_sem, line_send, line_recv, cross_send, cross_recv, near_send, near_recv,
-    halo_send, halo_recv, pot_send, pot_recv, word,
+    y_mat, mine, near_potential, centre, pot, cell_sem, given_sem, line_send, line_recv, cross_send, cross_recv,
+    near_send, near_recv, halo_send, halo_recv, pot_send, pot_recv, share_send, share_recv, word,
 ):
     s, g = lax.axis_index("slab"), lax.axis_index("grp")
     me = s * 16 + g
     pairs = slabs * 16
     below, above = s > 0, s < slabs - 1
-    from_below, from_above = below & (g < REACH), above & (g >= 16 - REACH)
+    works = g % 2 == 0
+    idle = jnp.logical_not(works)
+    first = g - g % 2
     middle = slabs // 2
     late, early, hub = s == middle - 1, s == middle, (s == middle - 2) & (g == HUB)
+    announce = word.at[0]
+    beside = word.at[1]
+    down = word.at[2]
+    go = word.at[3]
 
     def device(d):
         return (d // 16, d % 16)
+
+    def tell(semaphore, to):
+        pl.semaphore_signal(semaphore, 1, device_id=to, device_id_type=MESH)
 
     halves = [
         pltpu.make_async_copy(comp.at[4 * h : 4 * h + 4], cells.at[2 + 4 * h : 6 + 4 * h], cell_sem.at[h])
@@ -124,55 +134,68 @@
         half.start()
 
     barrier = pltpu.get_barrier_semaphore()
-    across = from_below | (from_above & (s != middle - 1) & (s != middle - 2))
-    other = jnp.where(g < REACH, s - 1, s + 1)
-    for k in FAR_FIRST + (0,):
-        peer = (g + k) % 16
-        if k:
-
-            @pl.when(jnp.logical_not(late))
-            def _():
-                pl.semaphore_signal(barrier, 1, device_id=(s, peer), device_id_type=MESH)
-
-        @pl.when(across)
-        def _():
-            pl.semaphore_signal(barrier, 1, device_id=(other, peer), device_id_type=MESH)
+
+    @pl.when(works & jnp.logical_not(late))
+    def _():
+        for k in FAR_FIRST:
+            tell(barrier, (s, (g + k) % 16))
+
+    @pl.when(works & below & (g < REACH))
+    def _():
+        for k in FAR_FIRST + (0,):
+            tell(barrier, (s - 1, (g + k) % 16))
+
+    @pl.when(works & above & (g >= 16 - WINDOW // 2) & (s != middle - 1) & (s != middle - 2))
+    def _():
+        for k in FAR_FIRST + (0,):
+            tell(barrier, (s + 1, (g + k) % 16))
 
     @pl.when(late)
     def _():
-        pl.semaphore_signal(barrier, 1, device_id=(s - 1, HUB), device_id_type=MESH)
-
-    @pl.when(early & (g >= REACH))
-    def _():
-        for to in range(16 - REACH, 16):
-            pl.semaphore_signal(barrier, 1, device_id=(s - 1, to), device_id_type=MESH)
+        tell(barrier, (s - 1, HUB))
+
+    @pl.when(early & (idle | (g >= REACH)))
+    def _():
+        for to in LOWER:
+            tell(barrier, (s - 1, to))
 
     load_guess.wait()
     packed = given.reshape(64, 32)
     lines[0:REACH] = jnp.zeros((REACH, 128), F32)
-    lines[REACH + 16 :] = jnp.zeros((REACH, 128), F32)
+    lines[REACH + 16 :] = jnp.zeros((REACH + 1, 128), F32)
     lines[REACH : REACH + 16] = jnp.concatenate(
         [packed[pl.ds(k, 16, stride=4), :] for k in range(4)], axis=1
     )
 
     def guess_up():
-        for to in range(REACH):
+        for to in UPPER:
             pltpu.make_async_remote_copy(
                 lines.at[16 + to : 21], beyond.at[0 : REACH - to, g], cross_send.at[0], cross_recv,
                 device_id=(s + 1, to), device_id_type=MESH,
             ).start()
 
+    def guess_down():
+        for to in LOWER:
+            pltpu.make_async_remote_copy(
+                lines.at[REACH : to - 4], beyond.at[21 - to : WINDOW, g], cross_send.at[1], cross_recv,
+                device_id=(s - 1, to), device_id_type=MESH,
+            ).start()
+
+    sends_down = (g == LOWER[0]) | (g == LOWER[1]) | (g == LOWER[2])
+
     @pl.when(late)
     def _():
-        pl.semaphore_wait(barrier, jnp.where(g < 16 - REACH, REACH, 16))
+        pl.semaphore_wait(barrier, jnp.where(sends_down, 16, 3))
         guess_up()
 
-        @pl.when(g >= 16 - REACH)
+        @pl.when(sends_down)
         def _():
             for k in range(16):
-                pl.semaphore_signal(
-                    word.at[0], 1, device_id=(s + 1, (g + k) % 16), device_id_type=MESH
-                )
+                tell(down, (s + 1, (g + k) % 16))
+
+        @pl.when(g == 15)
+        def _():
+            tell(down, (s + 1, 0))
 
     at, lane = iota((512, 128), 0), iota((512, 128), 1)
     hit = (at // 128 == lane // 32) & (at % 128 // 4 == lane % 32)
@@ -187,75 +210,89 @@
             parts.append(sum(sums[h, pl.ds(4 * half + j, 16, stride=8), :] for j in range(4)))
     wide = jnp.concatenate(split3(jnp.concatenate(parts, axis=1)), axis=0)
     means = jnp.dot(wide, gather[...], preferred_element_type=F32)
-    sources[REACH] = means[:16] + means[16:32] + means[32:]
+    means = means[:16] + means[16:32] + means[32:]
+    mine[...] = means
+
+    @pl.when(works)
+    def _():
+        sources[REACH] = means
 
     @pl.when(jnp.logical_not(late))
     def _():
-        asked = REACH * (above.astype(jnp.int32) + (below & jnp.logical_not(early)).astype(jnp.int32))
-        pl.semaphore_wait(barrier, 15 + asked + 16 * hub.astype(jnp.int32))
+        asked = 3 * (above.astype(jnp.int32) + (below & jnp.logical_not(early)).astype(jnp.int32))
+        pl.semaphore_wait(barrier, 7 + g % 2 + asked + 16 * hub.astype(jnp.int32))
 
     @pl.when(hub)
     def _():
         for to in range(16):
-            pl.semaphore_signal(word.at[1], 1, device_id=(s + 1, to), device_id_type=MESH)
-
-    pl.when(above & jnp.logical_not(late))(guess_up)
+            tell(go, (s + 1, to))
 
     near = []
-    for k in range(REACH, 0, -1):
-        for i, o in ((2 * k - 2, k), (2 * k - 1, -k)):
-            copy = pltpu.make_async_remote_copy(
-                sources.at[REACH], sources.at[REACH - o], near_send.at[i], near_recv.at[i],
-                device_id=device(me + o), device_id_type=MESH,
-            )
-            near.append((copy, o))
+    for i in (0, 5, 1, 4, 2, 3):
+        o = 2 * i - 6 + g % 2
+        copy = pltpu.make_async_remote_copy(
+            mine, sources.at[REACH - o], near_send.at[i], near_recv.at[REACH - o],
+            device_id=device(me + o), device_id_type=MESH,
+        )
+        goes = (me + o >= 0) & (me + o < pairs) & (o != 0)
+        near.append((copy, o, goes))
     halo = []
     for i, (o, src, dst) in enumerate(((1, comp.at[6:8], cells.at[0:2]), (-1, comp.at[0:2], cells.at[10:12]))):
         copy = pltpu.make_async_remote_copy(
             src, dst, halo_send.at[i], halo_recv.at[i], device_id=device(me + o), device_id_type=MESH
         )
-        halo.append((copy, o))
-
-    def goes(o):
-        return (me + o >= 0) & (me + o < pairs)
-
-    def comes(o):
-        return (me - o >= 0) & (me - o < pairs)
-
-    def guess_down():
-        for to in range(16 - REACH, 16):
-            pltpu.make_async_remote_copy(
-                lines.at[REACH : to - 5], beyond.at[21 - to : WINDOW, g], cross_send.at[1], cross_recv,
-                device_id=(s - 1, to), device_id_type=MESH,
-            ).start()
+        halo.append((copy, o, (me + o >= 0) & (me + o < pairs)))
 
     @pl.when(late)
     def _():
-        for copy, o in near + halo:
-            if o > 0:
-                pl.when(g + o > 15)(copy.start)
-        pl.semaphore_wait(word.at[1], 1)
-
-    pl.when(below & jnp.logical_not(early))(guess_down)
-    for k in FAR_FIRST:
-        to = (g + k) % 16
-        pltpu.make_async_remote_copy(
+        for copy, o, goes in near:
+            pl.when(g + o > 15)(copy.start)
+        pl.when(g == 15)(halo[0][0].start)
+        pl.semaphore_wait(go, 1)
+
+    for j in (4, 3, 5, 2, 6, 1, 7, 0):
+        to = (first + 2 * j) % 16
+        copy = pltpu.make_async_remote_copy(
             lines.at[pl.ds(to, WINDOW)], guesses.at[:, g], line_send, line_recv,
             device_id=(s, to), device_id_type=MESH,
-        ).start()
-    guesses[:, pl.ds(g, 1), :] = lines[pl.ds(g, WINDOW), :].reshape(WINDOW, 1, 128)
-    for copy, o in near + halo:
-        inside = (g + o >= 0) & (g + o < 16)
-        rest = jnp.logical_not(late) if o > 0 else jnp.logical_not(early)
-        pl.when(inside | (goes(o) & rest))(copy.start)
+        )
+        if j:
+            copy.start()
+        else:
+            pl.when(idle)(copy.start)
+    pl.when(above & jnp.logical_not(late))(guess_up)
+    pl.when(below & jnp.logical_not(early))(guess_down)
+    for copy, o, goes in near:
+        up, under = g + o > 15, g + o < 0
+        pl.when(goes & jnp.logical_not((up & late) | (under & early)))(copy.start)
+
+    @pl.when(works)
+    def _():
+        guesses[:, pl.ds(g, 1), :] = lines[pl.ds(g, WINDOW), :].reshape(WINDOW, 1, 128)
+        pl.semaphore_wait(beside, 1 + ((me > 0) & jnp.logical_not(early & (g == 0))).astype(jnp.int32))
+
+    @pl.when(idle)
+    def _():
+        tell(beside, (s, g - 1))
+
+        @pl.when((me < pairs - 1) & jnp.logical_not(late & (g == 15)))
+        def _():
+            tell(beside, device(me + 1))
+
+        for j in (4, 3, 5, 2, 6, 1, 7, 0):
+            tell(announce, (s, (first + 2 * j) % 16))
+
+    for copy, o, goes in halo:
+        apart = late & (g == 15) if o > 0 else early & (g == 0)
+        pl.when(goes & jnp.logical_not(apart))(copy.start)
 
     @pl.when(early)
     def _():
-        pl.semaphore_wait(word.at[0], REACH)
+        pl.semaphore_wait(down, 3 + (g == 0).astype(jnp.int32))
         guess_down()
-        for copy, o in near + halo:
-            if o < 0:
-                pl.when(g + o < 0)(copy.start)
+        for copy, o, goes in near:
+            pl.when(g + o < 0)(copy.start)
+        pl.when(g == 0)(halo[1][0].start)
 
     at, lane = iota((128, 512), 0), iota((128, 512), 1)
     hit = (lane // 128 == at // 32) & (lane % 128 // 4 == at % 32)
@@ -280,41 +317,79 @@
     lax.fori_loop(1, 7, lambda p, _: (chemical(p), 0)[1], 0)
     lax.fori_loop(2, 6, lambda f, _: (partial(f), 0)[1], 0)
 
-    lines_in = pltpu.make_async_remote_copy(
-        guesses.at[:, 0:15], guesses.at[:, 0:15], line_send, line_recv,
+    def counted(ref, send, recv):
+        return pltpu.make_async_remote_copy(
+            ref, ref, send, recv, device_id=(s, (g + 1) % 16), device_id_type=MESH
+        )
+
+    share = pltpu.make_async_remote_copy(
+        near_potential.at[16:64], near_potential.at[0:48], share_send, share_recv,
         device_id=(s, (g + 1) % 16), device_id_type=MESH,
     )
-    lines_in.wait_recv()
-    for there, spots in (
-        (from_below, [(j, slice(0, REACH - j)) for j in range(REACH)]),
-        (from_above, [(j, slice(21 - j, WINDOW)) for j in range(16 - REACH, 16)]),
-    ):
-        for j, spot in spots:
-
-            @pl.when(there & (g == j))
-            def _():
-                pltpu.make_async_remote_copy(
-                    beyond.at[spot], beyond.at[spot], cross_send.at[0], cross_recv,
-                    device_id=(s, (g + 1) % 16), device_id_type=MESH,
-                ).wait_recv()
-
-    for copy, o in near:
-        pl.when(comes(o))(copy.wait_recv)
-    place = g - REACH + iota((WINDOW * 16, 128), 0) // 16
-    start = jnp.where(
-        (place >= 0) & (place < 16), guesses[...].reshape(WINDOW * 16, 128), beyond[...].reshape(WINDOW * 16, 128)
-    )
-    potential = coarse_cycle(sources[...].reshape(WINDOW * 16, 128), start, me - REACH, pairs)
+
+    @pl.when(works)
+    def _():
+        counted(guesses.at[:, 0:15], line_send, line_recv).wait_recv()
+        for there, spots in (
+            (below, [(j, slice(0, REACH - j)) for j in UPPER]),
+            (above, [(j, slice(21 - j, WINDOW)) for j in LOWER]),
+        ):
+            for j, spot in spots:
+
+                @pl.when(there & (g == j))
+                def _():
+                    counted(beyond.at[spot], cross_send.at[0], cross_recv).wait_recv()
+
+        for k in range(WINDOW):
+            if k != REACH:
+                comes = (me - REACH + k >= 0) & (me - REACH + k < pairs)
+                pl.when(comes)(counted(mine, near_send.at[0], near_recv.at[k]).wait_recv)
+        place = g - REACH + iota((WINDOW * 16, 128), 0) // 16
+        start = jnp.where(
+            (place >= 0) & (place < 16), guesses[...].reshape(WINDOW * 16, 128), beyond[...].reshape(WINDOW * 16, 128)
+        )
+        potential = coarse_cycle(sources[...].reshape(WINDOW * 16, 128), start, me - REACH, pairs)
+        near_potential[...] = potential
+        centre[...] = potential[16:48].reshape(2, 16, 128)
+        pl.semaphore_wait(announce, 8)
+        share.start()
+        for k in FAR_FIRST:
+            to = (g + k) % 16
+            pltpu.make_async_remote_copy(
+                centre.at[:, to], pot.at[pl.ds(g, 2)], pot_send, pot_recv,
+                device_id=(s, to), device_id_type=MESH,
+            ).start()
+        pot[pl.ds(g, 2), :] = centre[:, pl.ds(g, 1), :].reshape(2, 128)
+
+    for copy, o, _ in halo:
+        pl.when((me - o >= 0) & (me - o < pairs))(copy.wait_recv)
+    zero = jnp.zeros((2, 128, 128), F32)
+
+    @pl.when(me == 0)
+    def _():
+        cells[0:2] = zero
+
+    @pl.when(me == pairs - 1)
+    def _():
+        cells[10:12] = zero
+
+    for p in (-1, 0, 7, 8):
+        chemical(p)
+
+    @pl.when(me == 0)
+    def _():
+        chem[0] = zero[0]
+
+    @pl.when(me == pairs - 1)
+    def _():
+        chem[9] = zero[0]
+
+    for f in (0, 1, 6, 7):
+        partial(f)
+
+    pl.when(idle)(share.wait_recv)
+    potential = near_potential[0:48]
     own = potential[16:32]
-    centre[...] = own
-    for k in FAR_FIRST:
-        to = (g + k) % 16
-        pltpu.make_async_remote_copy(
-            centre.at[pl.ds(to, 1)], pot.at[pl.ds(g, 1)], pot_send, pot_recv,
-            device_id=(s, to), device_id_type=MESH,
-        ).start()
-    pot[pl.ds(g, 1), :] = centre[pl.ds(g, 1), :]
-
     lane = iota((16, 128), 1)
     swapped = pltpu.roll(potential, 64, 1)
     before = jnp.where(lane < 64, swapped[:16], swapped[16:32]) - own
@@ -337,32 +412,6 @@
             for py in range(2)
         ]
 
-    for copy, o in halo:
-        pl.when(comes(o))(copy.wait_recv)
-    zero = jnp.zeros((2, 128, 128), F32)
-
-    @pl.when(me == 0)
-    def _():
-        cells[0:2] = zero
-
-    @pl.when(me == pairs - 1)
-    def _():
-        cells[10:12] = zero
-
-    for p in (-1, 0, 7, 8):
-        chemical(p)
-
-    @pl.when(me == 0)
-    def _():
-        chem[0] = zero[0]
-
-    @pl.when(me == pairs - 1)
-    def _():
-        chem[9] = zero[0]
-
-    for f in (0, 1, 6, 7):
-        partial(f)
-
     for px in range(2):
         rhs = jnp.concatenate(stacked(t0, 0, 256 * px) + stacked(t1, 0, 256 * px), 0)
         base = 0.08 * jnp.dot(y_mat[...], rhs, preferred_element_type=F32)
@@ -377,27 +426,36 @@
         out[4 * px + 2] += base
         out[4 * px + 3] += base + high
 
-    done = pltpu.make_async_remote_copy(
-        centre.at[pl.ds(0, 15)], pot.at[pl.ds(0, 15)], pot_send, pot_recv,
-        device_id=(s, (g + 1) % 16), device_id_type=MESH,
-    )
-    done.wait_recv()
+    @pl.when(works)
+    def _():
+        counted(pot.at[0:14], pot_send, pot_recv).wait_recv()
+
+    @pl.when(idle)
+    def _():
+        counted(pot.at[0:16], pot_send, pot_recv).wait_recv()
+
     packed = result.reshape(64, 32)
     for k in range(4):
         packed[pl.ds(k, 16, stride=4), :] = pot[:, 32 * k : 32 * k + 32]
-    done.wait_send()
-    lines_in.wait_send()
+
+    @pl.when(works)
+    def _():
+        counted(centre.at[:, 0:15], pot_send, pot_recv).wait_send()
+        share.wait_send()
+        counted(guesses.at[:, 0:7], line_send, line_recv).wait_send()
+
+    @pl.when(idle)
+    def _():
+        counted(guesses.at[:, 0:8], line_send, line_recv).wait_send()
+
     for i, there in ((0, above), (1, below)):
 
         @pl.when(there)
         def _():
-            pltpu.make_async_remote_copy(
-                lines.at[0:15], lines.at[0:15], cross_send.at[i], cross_recv,
-                device_id=(s, (g + 1) % 16), device_id_type=MESH,
-            ).wait_send()
-
-    for copy, o in near + halo:
-        pl.when(goes(o))(copy.wait_send)
+            counted(lines.at[0:9], cross_send.at[i], cross_recv).wait_send()
+
+    for copy, _, goes in near + halo:
+        pl.when(goes)(copy.wait_send)
 
 
 def deliver(fine, coarse, out, pot, sem):
@@ -425,7 +483,7 @@
         scratch_shapes=[
             pltpu.VMEM((12, 128, 128), F32),
             pltpu.VMEM((32, 2, 32), F32),
-            pltpu.VMEM((16 + 2 * REACH, 128), F32),
+            pltpu.VMEM((17 + 2 * REACH, 128), F32),
             pltpu.VMEM((WINDOW, 16, 128), F32),
             pltpu.VMEM((WINDOW, 16, 128), F32),
             pltpu.VMEM((WINDOW, 16, 128), F32),
@@ -435,6 +493,8 @@
             pltpu.VMEM((3, 128, 512), BF16),
             pltpu.VMEM((128, 192), BF16),
             pltpu.VMEM((16, 128), F32),
+            pltpu.VMEM((64, 128), F32),
+            pltpu.VMEM((2, 16, 128), F32),
             pltpu.VMEM((16, 128), F32),
             dma((2,)),
             dma,
@@ -442,13 +502,15 @@
             dma,
             dma((2,)),
             dma,
-            dma((2 * REACH,)),
-            dma((2 * REACH,)),
+            dma((6,)),
+            dma((WINDOW,)),
             dma((2,)),
             dma((2,)),
             dma,
             dma,
-            pltpu.SemaphoreType.REGULAR((2,)),
+            dma,
+            dma,
+            pltpu.SemaphoreType.REGULAR((4,)),
         ],
         compiler_params=pltpu.CompilerParams(
             collective_id=0, has_side_effects=True, vmem_limit_bytes=62 * 1024 * 1024

time: 24.3 us -> 22.9 us (0.942)
  the two profiles are of different devices: /device:TPU:193 before, /device:TPU:6 now
where the time goes in v4:
time: 22.9 us; the launch traced here: 22.8 us
  Pallas kernels  22.1 us (97%)
  between operations  0.64 us (3%)
    pallas_call x1, Pallas kernels, per_device(): pl.pallas_call(body, out_shape=(pltpu.VMEM((8, 128, 128), F32), pltpu.VME...  21.3 us
    pallas_call x1, Pallas kernels, per_device(): pl.pallas_call(deliver, out_shape=(jax.ShapeDtypeStruct(comp.shape, F32),...  0.81 us

profile of v4, /device:TPU:6, one launch (start us, length us, event | category | flops | bytes accessed | tf_op | source)
XLA Modules:
  0.0 22.8 jit_solution(7626476849052881487)
XLA Ops:
  0.6 21.3 %step.1 = (f32[8,128,128]{2,1,0:T(8,128)S(1)}, f32[32,2,32]{2,1,0:T(2,128)S(1)}) custom-call(f32[8,128,128]{2,1,0:T(8,128)} %refs_0_.1, f32[32,2,32]{2,1,0:T(2,128)} %refs_1_.1), custom_call_target="tpu_custom_call" | custom-call | tf_op jit(solution)/shard_map/step/pallas_call | solution.py:478
  22.0 0.8 %deliver.1 = (f32[8,128,128]{2,1,0:T(8,128)}, f32[32,2,32]{2,1,0:T(2,128)}) custom-call(f32[8,128,128]{2,1,0:T(8,128)S(1)} %get-tuple-element.4.fine, f32[32,2,32]{2,1,0:T(2,128)S(1)} %get-tuple-element.5.coarse), custom_call_target="tpu_custom_call" | custom-call | tf_op jit(solution)/shard_map/deliver/pallas_call | solution.py:520

commit v5 on v4

--- a/solution.py
+++ b/solution.py
@@ -35,51 +35,62 @@
     return high, mid, low
 
 
-def neighbours(v, first, last):
-    own = v[16:-16]
-    lane, row = iota(own.shape, 1), iota(own.shape, 0) % 16
-    a, b = lanes(own, 32), lanes(own, -32)
-    up = jnp.where(row < 15, rows(b, 1), 0.0)
-    down = jnp.where(row > 0, rows(a, -1), 0.0)
-    total = jnp.where(lane % 64 < 32, a + down, b + up)
-    total += jnp.where(lane % 32 < 31, lanes(own, 1), 0.0)
-    total += jnp.where(lane % 32 > 0, lanes(own, -1), 0.0)
-    h = pltpu.roll(v, 64, 1)
-    return total + h[16:-16] + jnp.where(lane < 64, h[:-32], h[32:])
-
-
 def coarse_cycle(source, guess, first_pair, pairs):
-    def inside(v, first):
-        pair = first_pair + first + iota(v.shape, 0) // 16
-        return jnp.where((pair >= 0) & (pair < pairs), v, 0.0)
-
-    def sweep(v, s):
-        return 0.2 * v[16:-16] + (0.8 / 6.5) * (s + neighbours(v, 0, 0))
-
-    guess = inside(guess, 0)
-    source = inside(source, 0)
-    edge = jnp.zeros((16, 128), F32)
-    pre = inside(sweep(jnp.concatenate([edge, guess, edge], 0), source), 0)
-    resid = inside(source[16:-16] + neighbours(pre, 0, 0) - 6.5 * pre[16:-16], 1)
-    lane = iota(resid.shape, 1)
-    t = resid + pltpu.roll(resid, 64, 1)
-    t = t + jnp.where(lane % 64 < 32, lanes(t, 32), lanes(t, -32))
-    t = t + jnp.where(lane % 2 < 1, lanes(t, 1), lanes(t, -1))
-    start = t * 0.05
-    c, first = start, 1
-    for _ in range(2):
-        own = c[16:-16]
-        lane, row = iota(own.shape, 1) % 32, iota(own.shape, 0) % 16
-        total = c[:-32] + c[32:]
-        total += jnp.where(row < 15, rows(own, 1), 0.0) + jnp.where(row > 0, rows(own, -1), 0.0)
-        total += jnp.where(lane < 30, lanes(own, 2), 0.0) + jnp.where(lane > 1, lanes(own, -2), 0.0)
-        first = first + 1
-        c = inside(0.2 * own + start[16 * (first - 1) : -16 * (first - 1)] + 0.1 * total, first)
-    mid = inside(pre[16 * first : -16 * first] + c, first)
-    mid = inside(sweep(mid, source[16 * (first + 1) : -16 * (first + 1)]), first + 1)
-    edge = jnp.zeros((16, 128), F32)
-    mid = jnp.concatenate([edge, mid, edge], 0)
-    return inside(sweep(mid, source[16 * (first + 1) : -16 * (first + 1)]), first + 1)
+    lane, row = iota((16, 128), 1), iota((16, 128), 0)
+    front, odd_row = lane < 64, lane % 64 >= 32
+    zero = jnp.zeros((16, 128), F32)
+    known = [(first_pair + k >= 0) & (first_pair + k < pairs) for k in range(WINDOW)]
+    inside = [jnp.where(k, 1.0, 0.0).astype(F32) for k in known]
+    guess = {k: jnp.where(known[k], guess[k], 0.0) for k in guess}
+    source = {k: jnp.where(known[k], source[k], 0.0) for k in source}
+
+    def above(v):
+        return jnp.where(row < 15, rows(v, 1), 0.0)
+
+    def under(v):
+        return jnp.where(row > 0, rows(v, -1), 0.0)
+
+    def neighbours(v, wanted):
+        swapped = {k: pltpu.roll(v[k], 64, 1) for k in v}
+        done = {}
+        for k in wanted:
+            line = v[k] + jnp.where(odd_row, under(v[k]), above(v[k]))
+            line = jnp.where(odd_row, lanes(line, -32), lanes(line, 32))
+            line += jnp.where(lane % 32 < 31, lanes(v[k], 1), 0.0)
+            line += jnp.where(lane % 32 > 0, lanes(v[k], -1), 0.0)
+            beside = jnp.where(front, swapped.get(k - 1, zero), swapped.get(k + 1, zero))
+            done[k] = line + swapped[k] + beside
+        return done
+
+    def sweep(v, wanted):
+        around = neighbours(v, wanted)
+        return {k: inside[k] * (0.2 * v[k] + (0.8 / 6.5) * (source[k] + around[k])) for k in wanted}
+
+    pre = sweep(guess, range(WINDOW))
+    places = range(1, WINDOW - 1)
+    around = neighbours(pre, places)
+    resid = jnp.concatenate(
+        [(0.05 * inside[k]) * (source[k] + around[k] - 6.5 * pre[k]) for k in places], 0
+    )
+    at, to = iota((256, 128), 0), iota((256, 128), 1)
+    cell = jnp.where((at % 32) // 2 == (to % 32) // 2, 1.0, 0.0).astype(BF16)
+    high, mid, low = split3(resid)
+    cells = jnp.dot(jnp.concatenate([high, mid], 1), cell, preferred_element_type=F32)
+    cells += jnp.dot(low, cell[:128], preferred_element_type=F32)
+    start = {k: cells[16 * (k - 1) : 16 * k] for k in places}
+    c = start
+    for sweeps in range(1, 3):
+        new = {}
+        for k in places[sweeps : len(places) - sweeps]:
+            v = c[k]
+            total = c[k - 1] + c[k + 1] + above(v) + under(v)
+            total += jnp.where(lane % 32 < 30, lanes(v, 2), 0.0) + jnp.where(lane % 32 > 1, lanes(v, -2), 0.0)
+            new[k] = inside[k] * (0.2 * v + start[k] + 0.1 * total)
+        c = new
+    v = {k: pre[k] + c[k] for k in c}
+    wanted = range(4, WINDOW - 4)
+    v = sweep(sweep(v, wanted), wanted)
+    return jnp.concatenate([v[k] for k in wanted], 0)
 
 
 def plane_neighbours(v):
@@ -159,10 +170,27 @@
         for to in LOWER:
             tell(barrier, (s - 1, to))
 
+    @pl.when(late)
+    def _():
+        receives = (g == LOWER[0]) | (g == LOWER[1]) | (g == LOWER[2])
+        pl.semaphore_wait(barrier, jnp.where(receives, 16, 3))
+
+        @pl.when(receives)
+        def _():
+            for k in FAR_FIRST + (0,):
+                tell(down, (s + 1, (g + k) % 16))
+
+        @pl.when(g == 15)
+        def _():
+            tell(down, (s + 1, 0))
+
+    lines[0:REACH] = jnp.zeros((REACH, 128), F32)
+    lines[REACH + 16 :] = jnp.zeros((REACH + 1, 128), F32)
+    at, lane = iota((512, 128), 0), iota((512, 128), 1)
+    hit = (at // 128 == lane // 32) & (at % 128 // 4 == lane % 32)
+    gather[...] = jnp.where(hit, 1.0 / 64, 0.0).astype(BF16)
     load_guess.wait()
     packed = given.reshape(64, 32)
-    lines[0:REACH] = jnp.zeros((REACH, 128), F32)
-    lines[REACH + 16 :] = jnp.zeros((REACH + 1, 128), F32)
     lines[REACH : REACH + 16] = jnp.concatenate(
         [packed[pl.ds(k, 16, stride=4), :] for k in range(4)], axis=1
     )
@@ -181,25 +209,10 @@
                 device_id=(s - 1, to), device_id_type=MESH,
             ).start()
 
-    sends_down = (g == LOWER[0]) | (g == LOWER[1]) | (g == LOWER[2])
-
     @pl.when(late)
     def _():
-        pl.semaphore_wait(barrier, jnp.where(sends_down, 16, 3))
         guess_up()
 
-        @pl.when(sends_down)
-        def _():
-            for k in range(16):
-                tell(down, (s + 1, (g + k) % 16))
-
-        @pl.when(g == 15)
-        def _():
-            tell(down, (s + 1, 0))
-
-    at, lane = iota((512, 128), 0), iota((512, 128), 1)
-    hit = (at // 128 == lane // 32) & (at % 128 // 4 == lane % 32)
-    gather[...] = jnp.where(hit, 1.0 / 64, 0.0).astype(BF16)
     for h in range(2):
         halves[h].wait()
         own = 2 + 4 * h
@@ -231,7 +244,7 @@
     for i in (0, 5, 1, 4, 2, 3):
         o = 2 * i - 6 + g % 2
         copy = pltpu.make_async_remote_copy(
-            mine, sources.at[REACH - o], near_send.at[i], near_recv.at[REACH - o],
+            mine, sources.at[REACH - o], near_send.at[i], near_recv,
             device_id=device(me + o), device_id_type=MESH,
         )
         goes = (me + o >= 0) & (me + o < pairs) & (o != 0)
@@ -250,6 +263,8 @@
         pl.when(g == 15)(halo[0][0].start)
         pl.semaphore_wait(go, 1)
 
+    pl.when(above & jnp.logical_not(late))(guess_up)
+    pl.when(below & jnp.logical_not(early))(guess_down)
     for j in (4, 3, 5, 2, 6, 1, 7, 0):
         to = (first + 2 * j) % 16
         copy = pltpu.make_async_remote_copy(
@@ -260,8 +275,6 @@
             copy.start()
         else:
             pl.when(idle)(copy.start)
-    pl.when(above & jnp.logical_not(late))(guess_up)
-    pl.when(below & jnp.logical_not(early))(guess_down)
     for copy, o, goes in near:
         up, under = g + o > 15, g + o < 0
         pl.when(goes & jnp.logical_not((up & late) | (under & early)))(copy.start)
@@ -340,15 +353,17 @@
                 def _():
                     counted(beyond.at[spot], cross_send.at[0], cross_recv).wait_recv()
 
-        for k in range(WINDOW):
-            if k != REACH:
-                comes = (me - REACH + k >= 0) & (me - REACH + k < pairs)
-                pl.when(comes)(counted(mine, near_send.at[0], near_recv.at[k]).wait_recv)
-        place = g - REACH + iota((WINDOW * 16, 128), 0) // 16
-        start = jnp.where(
-            (place >= 0) & (place < 16), guesses[...].reshape(WINDOW * 16, 128), beyond[...].reshape(WINDOW * 16, 128)
-        )
-        potential = coarse_cycle(sources[...].reshape(WINDOW * 16, 128), start, me - REACH, pairs)
+        lost = jnp.maximum(REACH - me, 0) + jnp.maximum(me + 7 - pairs, 0)
+        for less in (0, 1, 3, 5):
+
+            @pl.when(lost == less)
+            def _():
+                counted(sources.at[0 : WINDOW - 1 - less], near_send.at[0], near_recv).wait_recv()
+
+        start = {
+            k: jnp.where((g - REACH + k >= 0) & (g - REACH + k < 16), guesses[k], beyond[k]) for k in range(WINDOW)
+        }
+        potential = coarse_cycle({k: sources[k] for k in range(WINDOW)}, start, me - REACH, pairs)
         near_potential[...] = potential
         centre[...] = potential[16:48].reshape(2, 16, 128)
         pl.semaphore_wait(announce, 8)
@@ -428,6 +443,25 @@
 
     @pl.when(works)
     def _():
+        counted(guesses.at[:, 0:7], line_send, line_recv).wait_send()
+
+    @pl.when(idle)
+    def _():
+        counted(guesses.at[:, 0:8], line_send, line_recv).wait_send()
+
+    for i, there in ((0, above), (1, below)):
+
+        @pl.when(there)
+        def _():
+            counted(lines.at[0:9], cross_send.at[i], cross_recv).wait_send()
+
+    for copy, _, goes in near + halo:
+        pl.when(goes)(copy.wait_send)
+
+    @pl.when(works)
+    def _():
+        share.wait_send()
+        counted(centre.at[:, 0:15], pot_send, pot_recv).wait_send()
         counted(pot.at[0:14], pot_send, pot_recv).wait_recv()
 
     @pl.when(idle)
@@ -437,25 +471,6 @@
     packed = result.reshape(64, 32)
     for k in range(4):
         packed[pl.ds(k, 16, stride=4), :] = pot[:, 32 * k : 32 * k + 32]
-
-    @pl.when(works)
-    def _():
-        counted(centre.at[:, 0:15], pot_send, pot_recv).wait_send()
-        share.wait_send()
-        counted(guesses.at[:, 0:7], line_send, line_recv).wait_send()
-
-    @pl.when(idle)
-    def _():
-        counted(guesses.at[:, 0:8], line_send, line_recv).wait_send()
-
-    for i, there in ((0, above), (1, below)):
-
-        @pl.when(there)
-        def _():
-            counted(lines.at[0:9], cross_send.at[i], cross_recv).wait_send()
-
-    for copy, _, goes in near + halo:
-        pl.when(goes)(copy.wait_send)
 
 
 def deliver(fine, coarse, out, pot, sem):
@@ -503,7 +518,7 @@
             dma((2,)),
             dma,
             dma((6,)),
-            dma((WINDOW,)),
+            dma,
             dma((2,)),
             dma((2,)),
             dma,

time: 22.9 us -> 22.5 us (0.983)
  Pallas kernels: 22.1 us -> 21.7 us
    pallas_call x1, Pallas kernels: 21.3 us -> 20.9 us  [per_device(): pl.pallas_call(body, out_shape=(pltpu.VMEM((8, 128, 128), F32), pltpu.VME...]
where the time goes in v5:
time: 22.5 us; the launch traced here: 22.3 us
  Pallas kernels  21.7 us (96%)
  between operations  0.64 us (3%)
    pallas_call x1, Pallas kernels, per_device(): pl.pallas_call(body, out_shape=(pltpu.VMEM((8, 128, 128), F32), pltpu.VME...  20.9 us
    pallas_call x1, Pallas kernels, per_device(): pl.pallas_call(deliver, out_shape=(jax.ShapeDtypeStruct(comp.shape, F32),...  0.81 us

profile of v5, /device:TPU:6, one launch (start us, length us, event | category | flops | bytes accessed | tf_op | source)
XLA Modules:
  0.0 22.3 jit_solution(1499182299801406582)
XLA Ops:
  0.6 20.9 %step.1 = (f32[8,128,128]{2,1,0:T(8,128)S(1)}, f32[32,2,32]{2,1,0:T(2,128)S(1)}) custom-call(f32[8,128,128]{2,1,0:T(8,128)} %refs_0_.1, f32[32,2,32]{2,1,0:T(2,128)} %refs_1_.1), custom_call_target="tpu_custom_call" | custom-call | tf_op jit(solution)/shard_map/step/pallas_call | solution.py:493
  21.5 0.8 %deliver.1 = (f32[8,128,128]{2,1,0:T(8,128)}, f32[32,2,32]{2,1,0:T(2,128)}) custom-call(f32[8,128,128]{2,1,0:T(8,128)S(1)} %get-tuple-element.4.fine, f32[32,2,32]{2,1,0:T(2,128)S(1)} %get-tuple-element.5.coarse), custom_call_target="tpu_custom_call" | custom-call | tf_op jit(solution)/shard_map/deliver/pallas_call | solution.py:535

commit v6 on v5

--- a/solution.py
+++ b/solution.py
@@ -119,9 +119,11 @@
     me = s * 16 + g
     pairs = slabs * 16
     below, above = s > 0, s < slabs - 1
-    works = g % 2 == 0
+    first = g - g % 2
+    second = (s == 0) & (first == 0)
+    works = jnp.where(second, g == 1, g == first)
     idle = jnp.logical_not(works)
-    first = g - g % 2
+    base = s * 16 + first
     middle = slabs // 2
     late, early, hub = s == middle - 1, s == middle, (s == middle - 2) & (g == HUB)
     announce = word.at[0]
@@ -131,6 +133,9 @@
 
     def device(d):
         return (d // 16, d % 16)
+
+    def worker(pair):
+        return device(jnp.where(pair == 0, 1, pair))
 
     def tell(semaphore, to):
         pl.semaphore_signal(semaphore, 1, device_id=to, device_id_type=MESH)
@@ -228,12 +233,12 @@
 
     @pl.when(works)
     def _():
-        sources[REACH] = means
+        sources[REACH + g - first] = means
 
     @pl.when(jnp.logical_not(late))
     def _():
         asked = 3 * (above.astype(jnp.int32) + (below & jnp.logical_not(early)).astype(jnp.int32))
-        pl.semaphore_wait(barrier, 7 + g % 2 + asked + 16 * hub.astype(jnp.int32))
+        pl.semaphore_wait(barrier, 7 + idle.astype(jnp.int32) + asked + 16 * hub.astype(jnp.int32))
 
     @pl.when(hub)
     def _():
@@ -245,9 +250,10 @@
         o = 2 * i - 6 + g % 2
         copy = pltpu.make_async_remote_copy(
             mine, sources.at[REACH - o], near_send.at[i], near_recv,
-            device_id=device(me + o), device_id_type=MESH,
+            device_id=worker(me + o), device_id_type=MESH,
         )
-        goes = (me + o >= 0) & (me + o < pairs) & (o != 0)
+        itself = works & (me + o == base)
+        goes = (me + o >= 0) & (me + o < pairs) & jnp.logical_not(itself)
         near.append((copy, o, goes))
     halo = []
     for i, (o, src, dst) in enumerate(((1, comp.at[6:8], cells.at[0:2]), (-1, comp.at[0:2], cells.at[10:12]))):
@@ -269,7 +275,7 @@
         to = (first + 2 * j) % 16
         copy = pltpu.make_async_remote_copy(
             lines.at[pl.ds(to, WINDOW)], guesses.at[:, g], line_send, line_recv,
-            device_id=(s, to), device_id_type=MESH,
+            device_id=worker(s * 16 + to), device_id_type=MESH,
         )
         if j:
             copy.start()
@@ -281,19 +287,22 @@
 
     @pl.when(works)
     def _():
-        guesses[:, pl.ds(g, 1), :] = lines[pl.ds(g, WINDOW), :].reshape(WINDOW, 1, 128)
-        pl.semaphore_wait(beside, 1 + ((me > 0) & jnp.logical_not(early & (g == 0))).astype(jnp.int32))
+        guesses[:, pl.ds(g, 1), :] = lines[pl.ds(first, WINDOW), :].reshape(WINDOW, 1, 128)
+        alone = (early & (g == 0)) | ((s == 0) & ((g == 1) | (g == 2)))
+        pl.semaphore_wait(beside, jnp.where(alone, 1, 2))
 
     @pl.when(idle)
     def _():
-        tell(beside, (s, g - 1))
+        @pl.when(g > 0)
+        def _():
+            tell(beside, (s, g - 1))
 
         @pl.when((me < pairs - 1) & jnp.logical_not(late & (g == 15)))
         def _():
             tell(beside, device(me + 1))
 
         for j in (4, 3, 5, 2, 6, 1, 7, 0):
-            tell(announce, (s, (first + 2 * j) % 16))
+            tell(announce, worker(s * 16 + (first + 2 * j) % 16))
 
     for copy, o, goes in halo:
         apart = late & (g == 15) if o > 0 else early & (g == 0)
@@ -336,8 +345,8 @@
         )
 
     share = pltpu.make_async_remote_copy(
-        near_potential.at[16:64], near_potential.at[0:48], share_send, share_recv,
-        device_id=(s, (g + 1) % 16), device_id_type=MESH,
+        near_potential.at[pl.ds(16 * (1 + first - g), 48)], near_potential.at[0:48], share_send, share_recv,
+        device_id=(s, 2 * first + 1 - g), device_id_type=MESH,
     )
 
     @pl.when(works)
@@ -353,7 +362,7 @@
                 def _():
                     counted(beyond.at[spot], cross_send.at[0], cross_recv).wait_recv()
 
-        lost = jnp.maximum(REACH - me, 0) + jnp.maximum(me + 7 - pairs, 0)
+        lost = jnp.maximum(REACH - base, 0) + jnp.maximum(base + 7 - pairs, 0)
         for less in (0, 1, 3, 5):
 
             @pl.when(lost == less)
@@ -361,9 +370,9 @@
                 counted(sources.at[0 : WINDOW - 1 - less], near_send.at[0], near_recv).wait_recv()
 
         start = {
-            k: jnp.where((g - REACH + k >= 0) & (g - REACH + k < 16), guesses[k], beyond[k]) for k in range(WINDOW)
+            k: jnp.where((first - REACH + k >= 0) & (first - REACH + k < 16), guesses[k], beyond[k]) for k in range(WINDOW)
         }
-        potential = coarse_cycle({k: sources[k] for k in range(WINDOW)}, start, me - REACH, pairs)
+        potential = coarse_cycle({k: sources[k] for k in range(WINDOW)}, start, base - REACH, pairs)
         near_potential[...] = potential
         centre[...] = potential[16:48].reshape(2, 16, 128)
         pl.semaphore_wait(announce, 8)
@@ -371,10 +380,10 @@
         for k in FAR_FIRST:
             to = (g + k) % 16
             pltpu.make_async_remote_copy(
-                centre.at[:, to], pot.at[pl.ds(g, 2)], pot_send, pot_recv,
+                centre.at[:, to], pot.at[pl.ds(first, 2)], pot_send, pot_recv,
                 device_id=(s, to), device_id_type=MESH,
             ).start()
-        pot[pl.ds(g, 2), :] = centre[:, pl.ds(g, 1), :].reshape(2, 128)
+        pot[pl.ds(first, 2), :] = centre[:, pl.ds(g, 1), :].reshape(2, 128)
 
     for copy, o, _ in halo:
         pl.when((me - o >= 0) & (me - o < pairs))(copy.wait_recv)
@@ -403,7 +412,7 @@
         partial(f)
 
     pl.when(idle)(share.wait_recv)
-    potential = near_potential[0:48]
+    potential = near_potential[pl.ds(jnp.where(works, 16 * (g - first), 0), 48), :]
     own = potential[16:32]
     lane = iota((16, 128), 1)
     swapped = pltpu.roll(potential, 64, 1)

time: 22.5 us -> 22.5 us (level)
  no operation moved by 1% of the time
where the time goes in v6:
time: 22.5 us; the launch traced here: 22.3 us
  Pallas kernels  21.7 us (96%)
  between operations  0.64 us (3%)
    pallas_call x1, Pallas kernels, per_device(): pl.pallas_call(body, out_shape=(pltpu.VMEM((8, 128, 128), F32), pltpu.VME...  20.9 us
    pallas_call x1, Pallas kernels, per_device(): pl.pallas_call(deliver, out_shape=(jax.ShapeDtypeStruct(comp.shape, F32),...  0.81 us

profile of v6, /device:TPU:6, one launch (start us, length us, event | category | flops | bytes accessed | tf_op | source)
XLA Modules:
  0.0 22.3 jit_solution(5594026828155624588)
XLA Ops:
  0.6 20.9 %step.1 = (f32[8,128,128]{2,1,0:T(8,128)S(1)}, f32[32,2,32]{2,1,0:T(2,128)S(1)}) custom-call(f32[8,128,128]{2,1,0:T(8,128)} %refs_0_.1, f32[32,2,32]{2,1,0:T(2,128)} %refs_1_.1), custom_call_target="tpu_custom_call" | custom-call | tf_op jit(solution)/shard_map/step/pallas_call | solution.py:502
  21.5 0.8 %deliver.1 = (f32[8,128,128]{2,1,0:T(8,128)}, f32[32,2,32]{2,1,0:T(2,128)}) custom-call(f32[8,128,128]{2,1,0:T(8,128)S(1)} %get-tuple-element.4.fine, f32[32,2,32]{2,1,0:T(2,128)S(1)} %get-tuple-element.5.coarse), custom_call_target="tpu_custom_call" | custom-call | tf_op jit(solution)/shard_map/deliver/pallas_call | solution.py:544

commit v7 on v6

--- a/solution.py
+++ b/solution.py
@@ -93,6 +93,14 @@
     return jnp.concatenate([v[k] for k in wanted], 0)
 
 
+def three(potential, which):
+    lane = iota((16, 128), 1)
+    pair = [potential[16 * k : 16 * k + 16] for k in range(4)]
+    own = jnp.where(which == 0, pair[1], pair[2])
+    last, first = jnp.where(which == 0, pair[0], pair[1]), jnp.where(which == 0, pair[2], pair[3])
+    return jnp.concatenate([own, jnp.where(lane < 64, first, last)], 0)
+
+
 def plane_neighbours(v):
     row, lane = iota(v.shape, 0), iota(v.shape, 1)
     total = jnp.where(row < 127, rows(v, 1), 0.0) + jnp.where(row > 0, rows(v, -1), 0.0)
@@ -345,7 +353,7 @@
         )
 
     share = pltpu.make_async_remote_copy(
-        near_potential.at[pl.ds(16 * (1 + first - g), 48)], near_potential.at[0:48], share_send, share_recv,
+        near_potential.at[32:64], near_potential.at[0:32], share_send, share_recv,
         device_id=(s, 2 * first + 1 - g), device_id_type=MESH,
     )
 
@@ -373,7 +381,8 @@
             k: jnp.where((first - REACH + k >= 0) & (first - REACH + k < 16), guesses[k], beyond[k]) for k in range(WINDOW)
         }
         potential = coarse_cycle({k: sources[k] for k in range(WINDOW)}, start, base - REACH, pairs)
-        near_potential[...] = potential
+        near_potential[0:32] = three(potential, g - first)
+        near_potential[32:64] = three(potential, 1 + first - g)
         centre[...] = potential[16:48].reshape(2, 16, 128)
         pl.semaphore_wait(announce, 8)
         share.start()
@@ -412,12 +421,11 @@
         partial(f)
 
     pl.when(idle)(share.wait_recv)
-    potential = near_potential[pl.ds(jnp.where(works, 16 * (g - first), 0), 48), :]
-    own = potential[16:32]
+    own, edges = near_potential[0:16], near_potential[16:32]
     lane = iota((16, 128), 1)
-    swapped = pltpu.roll(potential, 64, 1)
-    before = jnp.where(lane < 64, swapped[:16], swapped[16:32]) - own
-    after = jnp.where(lane < 64, swapped[16:32], swapped[32:]) - own
+    swapped, edges = pltpu.roll(own, 64, 1), pltpu.roll(edges, 64, 1)
+    before = jnp.where(lane < 64, edges, swapped) - own
+    after = jnp.where(lane < 64, swapped, edges) - own
     left = jnp.where(lane % 32 > 0, lanes(own, -1), 0.0) - own
     right = jnp.where(lane % 32 < 31, lanes(own, 1), 0.0) - own
     t0 = jnp.dot(

time: 22.5 us -> 22.4 us (level)
  no operation moved by 1% of the time
where the time goes in v7:
time: 22.4 us; the launch traced here: 22.2 us
  Pallas kernels  21.6 us (96%)
  between operations  0.64 us (3%)
    pallas_call x1, Pallas kernels, per_device(): pl.pallas_call(body, out_shape=(pltpu.VMEM((8, 128, 128), F32), pltpu.VME...  20.8 us
    pallas_call x1, Pallas kernels, per_device(): pl.pallas_call(deliver, out_shape=(jax.ShapeDtypeStruct(comp.shape, F32),...  0.81 us

profile of v7, /device:TPU:6, one launch (start us, length us, event | category | flops | bytes accessed | tf_op | source)
XLA Modules:
  0.0 22.2 jit_solution(9777537830714942823)
XLA Ops:
  0.6 20.8 %step.1 = (f32[8,128,128]{2,1,0:T(8,128)S(1)}, f32[32,2,32]{2,1,0:T(2,128)S(1)}) custom-call(f32[8,128,128]{2,1,0:T(8,128)} %refs_0_.1, f32[32,2,32]{2,1,0:T(2,128)} %refs_1_.1), custom_call_target="tpu_custom_call" | custom-call | tf_op jit(solution)/shard_map/step/pallas_call | solution.py:510
  21.4 0.8 %deliver.1 = (f32[8,128,128]{2,1,0:T(8,128)}, f32[32,2,32]{2,1,0:T(2,128)}) custom-call(f32[8,128,128]{2,1,0:T(8,128)S(1)} %get-tuple-element.4.fine, f32[32,2,32]{2,1,0:T(2,128)S(1)} %get-tuple-element.5.coarse), custom_call_target="tpu_custom_call" | custom-call | tf_op jit(solution)/shard_map/deliver/pallas_call | solution.py:552

commit v8 on v6

--- a/solution.py
+++ b/solution.py
@@ -377,8 +377,8 @@
         centre[...] = potential[16:48].reshape(2, 16, 128)
         pl.semaphore_wait(announce, 8)
         share.start()
-        for k in FAR_FIRST:
-            to = (g + k) % 16
+        for k, close in zip(FAR_FIRST, reversed(FAR_FIRST)):
+            to = (g + jnp.where(early, close, k)) % 16
             pltpu.make_async_remote_copy(
                 centre.at[:, to], pot.at[pl.ds(first, 2)], pot_send, pot_recv,
                 device_id=(s, to), device_id_type=MESH,

time: 22.5 us -> 22.5 us (level)
  no operation moved by 1% of the time
where the time goes in v8:
time: 22.5 us; the launch traced here: 22.3 us
  Pallas kernels  21.7 us (96%)
  between operations  0.64 us (3%)
    pallas_call x1, Pallas kernels, per_device(): pl.pallas_call(body, out_shape=(pltpu.VMEM((8, 128, 128), F32), pltpu.VME...  20.9 us
    pallas_call x1, Pallas kernels, per_device(): pl.pallas_call(deliver, out_shape=(jax.ShapeDtypeStruct(comp.shape, F32),...  0.81 us

profile of v8, /device:TPU:6, one launch (start us, length us, event | category | flops | bytes accessed | tf_op | source)
XLA Modules:
  0.0 22.3 jit_solution(9537734705011210592)
XLA Ops:
  0.6 20.9 %step.1 = (f32[8,128,128]{2,1,0:T(8,128)S(1)}, f32[32,2,32]{2,1,0:T(2,128)S(1)}) custom-call(f32[8,128,128]{2,1,0:T(8,128)} %refs_0_.1, f32[32,2,32]{2,1,0:T(2,128)} %refs_1_.1), custom_call_target="tpu_custom_call" | custom-call | tf_op jit(solution)/shard_map/step/pallas_call | solution.py:502
  21.5 0.8 %deliver.1 = (f32[8,128,128]{2,1,0:T(8,128)}, f32[32,2,32]{2,1,0:T(2,128)}) custom-call(f32[8,128,128]{2,1,0:T(8,128)S(1)} %get-tuple-element.4.fine, f32[32,2,32]{2,1,0:T(2,128)S(1)} %get-tuple-element.5.coarse), custom_call_target="tpu_custom_call" | custom-call | tf_op jit(solution)/shard_map/deliver/pallas_call | solution.py:544
